TPU v7x, 128 devices: a whole 4x4x4 slice. The times are simulated.
128 devices in a mesh: dp: 16 (over x, y_hi, core), tensor: 8 (over z, y_lo).
Axes of the slice: x: 4, y: 4 (y_hi: 2, y_lo: 2; y = y_hi * 2 + y_lo), z: 4, core: 2. Of those that a mesh axis runs over, the one named last changes fastest.
Arguments:
- tokens: bfloat16 [16384, 1536], P(('dp', 'tensor')), may hold values from -6 to 6
- gain_mix: bfloat16 [1536], P('dp'), may hold values from 0.099609375 to 1.8984375
- in_weight: bfloat16 [1536, 3, 1536], P('dp', None, 'tensor'), may hold values from -0.15625 to 0.15625
- conv_kernel: bfloat16 [3, 1536], P(None, 'tensor'), may hold values from -3.5 to 3.5
- out_weight: bfloat16 [1536, 1536], P('tensor', 'dp'), may hold values from -0.15625 to 0.15625
- gain_ffn: bfloat16 [1536], P('dp'), may hold values from 0.099609375 to 1.8984375
- gate_weight: bfloat16 [1536, 6912], P('dp', 'tensor'), may hold values from -0.15625 to 0.15625
- up_weight: bfloat16 [1536, 6912], P('dp', 'tensor'), may hold values from -0.15625 to 0.15625
- down_weight: bfloat16 [6912, 1536], P('tensor', 'dp'), may hold values from -0.078125 to 0.078125
- lengths: int32 [16], P('dp'), may hold values from 256 to 1024, as said below
- cotangent: bfloat16 [16384, 1536], P(('dp', 'tensor')), may hold values from -6 to 6
Outputs:
- layer_out: bfloat16 [16384, 1536], P(('dp', 'tensor'))
- tokens_grad: bfloat16 [16384, 1536], P(('dp', 'tensor'))
- gain_mix_grad: float32 [1536], P(('dp', 'tensor'))
- in_grad: float32 [1536, 3, 1536], P('dp', None, 'tensor')
- kernel_grad: float32 [3, 1536], P(None, ('dp', 'tensor'))
- out_grad: float32 [1536, 1536], P('tensor', 'dp')
- gain_ffn_grad: float32 [1536], P(('dp', 'tensor'))
- gate_grad: float32 [1536, 6912], P('dp', 'tensor')
- up_grad: float32 [1536, 6912], P('dp', 'tensor')
- down_grad: float32 [6912, 1536], P('tensor', 'dp')
Inputs may be any that keep to these rules, and one draw needn't show every extreme that they name: `lengths`: lengths run from 256 to 1024; at least 4 sequences have length 1024.
All inputs are finite; a program needn't handle non-finite values.
Results may differ from a plain program's by a relative error of at most 0.025.
Values may be sent and summed in bfloat16 or wider, within the bound.
A program may use at most 128 MiB of HBM per device.

v0:
```python
import jax
import jax.numpy as jnp
from jax import lax
from jax.sharding import PartitionSpec as P

epsilon = 1e-05


def delay(values, steps, seq_count):
    shaped = values.reshape(seq_count, -1, values.shape[-1])
    moved = jnp.pad(shaped, ((0, 0), (steps, 0), (0, 0)))[:, : shaped.shape[1]]
    return moved.reshape(values.shape)


def advance(values, steps, seq_count):
    shaped = values.reshape(seq_count, -1, values.shape[-1])
    moved = jnp.pad(shaped, ((0, 0), (0, steps), (0, 0)))[:, steps:]
    return moved.reshape(values.shape)


def norm_backward_rule(gradient_of_normalized, centered_input, inverse_root, gain_widened):
    weighted_rows = gain_widened * gradient_of_normalized
    return inverse_root * (
        weighted_rows
        - centered_input * jnp.mean(weighted_rows * centered_input, axis=1, keepdims=True)
    )


def per_device(
    tokens,
    gain_mix,
    in_weight,
    conv_kernel,
    out_weight,
    gain_ffn,
    gate_weight,
    up_weight,
    down_weight,
    lengths,
    cotangent,
):
    tensor_count = lax.axis_size("tensor")
    tensor_index = lax.axis_index("tensor")
    row_count = tokens.shape[0]
    seq_count = lengths.shape[0]
    group_rows = row_count * tensor_count
    seq_slots = group_rows // seq_count
    channels = conv_kernel.shape[1]
    row_start = tensor_index * row_count
    slot_index = row_start + jnp.arange(row_count)
    seq_of = slot_index // seq_slots
    position = slot_index % seq_slots
    picked = seq_of[:, None] == jnp.arange(seq_count)[None, :]
    seq_length = jnp.sum(jnp.where(picked, lengths[None, :], 0), axis=1)
    live_mask = (position < seq_length).astype(jnp.float32)[:, None]
    w_in, mixer_gain_value, w_out = (
        lax.all_gather(in_weight, "dp", axis=0, tiled=True),
        lax.all_gather(gain_mix, "dp", axis=0, tiled=True),
        lax.all_gather(out_weight, "dp", axis=1, tiled=True),
    )
    w_gate, w_up, g_ffn, w_down = (
        lax.all_gather(gate_weight, "dp", axis=0, tiled=True),
        lax.all_gather(up_weight, "dp", axis=0, tiled=True),
        lax.all_gather(gain_ffn, "dp", axis=0, tiled=True),
        lax.all_gather(down_weight, "dp", axis=1, tiled=True),
    )
    ffn_gain_wide = g_ffn.astype(jnp.float32)
    token_rows_wide = tokens.astype(jnp.float32)
    first_inverse_root = lax.rsqrt(
        jnp.mean(token_rows_wide * token_rows_wide, axis=1, keepdims=True) + epsilon
    )
    first_centered_input = token_rows_wide * first_inverse_root
    normalized_rows = (first_centered_input * mixer_gain_value.astype(jnp.float32)).astype(
        jnp.bfloat16
    )
    normed_all = lax.all_gather(normalized_rows, "tensor", axis=0, tiled=True)
    projected = jnp.einsum("td,dkc->tkc", normed_all, w_in, preferred_element_type=jnp.float32)
    b_gate = projected[:, 0]
    c_gate = projected[:, 1]
    value_ch = projected[:, 2]
    kernel_f = conv_kernel.astype(jnp.float32)
    bx_prod = b_gate * value_ch
    bx_one = delay(bx_prod, 1, seq_count)
    bx_two = delay(bx_prod, 2, seq_count)
    conv_sum = kernel_f[0] * bx_prod + kernel_f[1] * bx_one + kernel_f[2] * bx_two
    mixed = (c_gate * conv_sum).astype(jnp.bfloat16)
    mixer_part = jnp.dot(mixed, w_out, preferred_element_type=jnp.float32)
    mixer_rows = lax.psum_scatter(mixer_part, "tensor", scatter_dimension=0, tiled=True)
    residual_stream = token_rows_wide + mixer_rows
    second_inverse_root = lax.rsqrt(
        jnp.mean(residual_stream * residual_stream, axis=1, keepdims=True) + epsilon
    )
    second_centered_input = residual_stream * second_inverse_root
    second_normalized_rows = (second_centered_input * ffn_gain_wide).astype(jnp.bfloat16)
    normed_two_all = lax.all_gather(second_normalized_rows, "tensor", axis=0, tiled=True)
    gate_pre = jnp.dot(normed_two_all, w_gate, preferred_element_type=jnp.float32)
    up_pre = jnp.dot(normed_two_all, w_up, preferred_element_type=jnp.float32)
    sig_gate = jax.nn.sigmoid(gate_pre)
    silu_gate = gate_pre * sig_gate
    hidden_act = (silu_gate * up_pre).astype(jnp.bfloat16)
    ffn_part = jnp.dot(hidden_act, w_down, preferred_element_type=jnp.float32)
    ffn_rows = lax.psum_scatter(
        ffn_part.astype(jnp.bfloat16), "tensor", scatter_dimension=0, tiled=True
    ).astype(jnp.float32)
    layer_out = (live_mask * (residual_stream + ffn_rows)).astype(jnp.bfloat16)
    back_in, backward_mixer_gain, back_out, back_gate, back_up, back_gffn, back_down = (
        lax.all_gather(in_weight, "dp", axis=0, tiled=True),
        lax.all_gather(gain_mix, "dp", axis=0, tiled=True),
        lax.all_gather(out_weight, "dp", axis=1, tiled=True),
        lax.all_gather(gate_weight, "dp", axis=0, tiled=True),
        lax.all_gather(up_weight, "dp", axis=0, tiled=True),
        lax.all_gather(gain_ffn, "dp", axis=0, tiled=True),
        lax.all_gather(down_weight, "dp", axis=1, tiled=True),
    )
    backward_ffn_gain_wide = back_gffn.astype(jnp.float32)
    output_gradient = live_mask * cotangent.astype(jnp.float32)
    grad_out_all = lax.all_gather(
        output_gradient.astype(jnp.bfloat16), "tensor", axis=0, tiled=True
    )
    down_full = jnp.einsum(
        "tf,td->fd", hidden_act, grad_out_all, preferred_element_type=jnp.float32
    )
    grad_act = jnp.einsum("td,fd->tf", grad_out_all, back_down, preferred_element_type=jnp.float32)
    grad_gate = (grad_act * up_pre * sig_gate * (1.0 + gate_pre * (1.0 - sig_gate))).astype(
        jnp.bfloat16
    )
    grad_up = (grad_act * silu_gate).astype(jnp.bfloat16)
    gate_full = jnp.einsum(
        "td,tf->df", normed_two_all, grad_gate, preferred_element_type=jnp.float32
    )
    up_full = jnp.einsum("td,tf->df", normed_two_all, grad_up, preferred_element_type=jnp.float32)
    grad_normed_two = jnp.einsum(
        "tf,df->td", grad_gate, back_gate, preferred_element_type=jnp.float32
    )
    grad_normed_two = grad_normed_two + jnp.einsum(
        "tf,df->td", grad_up, back_up, preferred_element_type=jnp.float32
    )
    second_gradient_rows = lax.psum_scatter(
        grad_normed_two.astype(jnp.bfloat16), "tensor", scatter_dimension=0, tiled=True
    ).astype(jnp.float32)
    ffn_gain_share = jnp.sum(second_gradient_rows * second_centered_input, axis=0)
    residual_gradient = output_gradient + norm_backward_rule(
        second_gradient_rows, second_centered_input, second_inverse_root, backward_ffn_gain_wide
    )
    grad_branch_all = lax.all_gather(
        residual_gradient.astype(jnp.bfloat16), "tensor", axis=0, tiled=True
    )
    gate_grad, up_grad, down_grad = (
        lax.psum_scatter(
            gate_full.astype(jnp.bfloat16), "dp", scatter_dimension=0, tiled=True
        ).astype(jnp.float32),
        lax.psum_scatter(
            up_full.astype(jnp.bfloat16), "dp", scatter_dimension=0, tiled=True
        ).astype(jnp.float32),
        lax.psum_scatter(
            down_full.astype(jnp.bfloat16), "dp", scatter_dimension=1, tiled=True
        ).astype(jnp.float32),
    )
    out_full = jnp.einsum("tc,td->cd", mixed, grad_branch_all, preferred_element_type=jnp.float32)
    grad_mixed = jnp.einsum(
        "td,cd->tc", grad_branch_all, back_out, preferred_element_type=jnp.float32
    )
    grad_c = grad_mixed * conv_sum
    grad_conv = grad_mixed * c_gate
    grad_bx = (
        kernel_f[0] * grad_conv
        + kernel_f[1] * advance(grad_conv, 1, seq_count)
        + kernel_f[2] * advance(grad_conv, 2, seq_count)
    )
    kernel_part = jnp.stack(
        [
            jnp.sum(grad_conv * bx_prod, axis=0),
            jnp.sum(grad_conv * bx_one, axis=0),
            jnp.sum(grad_conv * bx_two, axis=0),
        ],
        axis=0,
    )
    grad_projected = jnp.stack([grad_bx * value_ch, grad_c, grad_bx * b_gate], axis=1).astype(
        jnp.bfloat16
    )
    in_full = jnp.einsum(
        "td,tkc->dkc", normed_all, grad_projected, preferred_element_type=jnp.float32
    )
    gradient_of_normalized = jnp.einsum(
        "tkc,dkc->td", grad_projected, back_in, preferred_element_type=jnp.float32
    )
    first_gradient_rows = lax.psum_scatter(
        gradient_of_normalized.astype(jnp.bfloat16), "tensor", scatter_dimension=0, tiled=True
    ).astype(jnp.float32)
    mixer_gain_share = jnp.sum(first_gradient_rows * first_centered_input, axis=0)
    tokens_grad = (
        residual_gradient
        + norm_backward_rule(
            first_gradient_rows,
            first_centered_input,
            first_inverse_root,
            backward_mixer_gain.astype(jnp.float32),
        )
    ).astype(jnp.bfloat16)
    in_grad, out_grad = (
        lax.psum_scatter(
            in_full.astype(jnp.bfloat16), "dp", scatter_dimension=0, tiled=True
        ).astype(jnp.float32),
        lax.psum_scatter(
            out_full.astype(jnp.bfloat16), "dp", scatter_dimension=1, tiled=True
        ).astype(jnp.float32),
    )
    kernel_wide = lax.dynamic_update_slice(
        jnp.zeros((3, channels * tensor_count), jnp.float32),
        kernel_part,
        (0, tensor_index * channels),
    )
    gain_mix_grad, gain_ffn_grad, kernel_grad = (
        lax.psum_scatter(mixer_gain_share, ("dp", "tensor"), scatter_dimension=0, tiled=True),
        lax.psum_scatter(ffn_gain_share, ("dp", "tensor"), scatter_dimension=0, tiled=True),
        lax.psum_scatter(kernel_wide, ("dp", "tensor"), scatter_dimension=1, tiled=True),
    )
    return (
        layer_out,
        tokens_grad,
        gain_mix_grad,
        in_grad,
        kernel_grad,
        out_grad,
        gain_ffn_grad,
        gate_grad,
        up_grad,
        down_grad,
    )


def solution(mesh):
    placed = (
        P(("dp", "tensor"), None),
        P("dp"),
        P("dp", None, "tensor"),
        P(None, "tensor"),
        P("tensor", "dp"),
        P("dp"),
        P("dp", "tensor"),
        P("dp", "tensor"),
        P("tensor", "dp"),
        P("dp"),
        P(("dp", "tensor"), None),
    )
    return jax.shard_map(
        per_device,
        mesh=mesh,
        in_specs=placed,
        out_specs=(
            P(("dp", "tensor"), None),
            P(("dp", "tensor"), None),
            P(("dp", "tensor")),
            P("dp", None, "tensor"),
            P(None, ("dp", "tensor")),
            P("tensor", "dp"),
            P(("dp", "tensor")),
            P("dp", "tensor"),
            P("dp", "tensor"),
            P("tensor", "dp"),
        ),
        check_vma=False,
    )
```

profile of v0, /device:TPU:30, one launch (start us, length us, event | category | flops | bytes accessed | tf_op | source)
XLA Modules:
  0.0 1279.7 jit_solution(11833805110307657412)
XLA Ops:
  7.2 1.7 copy.24
  12.6 31.3 %all-reduce.10 = (bf16[1536]{0:T(1024)(128)(2,1)S(1)}, bf16[1536]{0:T(1024)(128)(2,1)}) all-reduce(bf16[1536]{0:T(1024)(128)(2,1)S(1)} %dynamic-update-slice, bf16[1536]{0:T(1024)(128)(2,1)S(1)} %dynamic-update-slice.1), channel_id=1, replica_groups=mesh['dp'=16,'tensor'=8] {'dp'}, use_global_device_ids=true, to_apply=%add.4 | all-reduce | flops 3072 | bytes 12288
  45.1 1.9 fusion.24
  48.0 1.4 fusion.40
  49.4 28.9 %all_gather.43 = bf16[192,1536]{0,1:T(8,128)(2,1)} all-gather(bf16[192,96]{0,1:T(8,128)(2,1)S(1)} %copy.26), channel_id=1, replica_groups=mesh['dp'=16,'tensor'=8] {'dp'}, dimensions={1}, use_global_device_ids=true | all-gather | bytes 626688 | tf_op jit(solution)/shard_map/all_gather | solution.py:59
  78.3 5.5 copy.25
  83.8 53.1 %all-gather.9.cloned.1.call-done = bf16[1024,1536]{1,0:T(8,128)(2,1)} async-done(((bf16[128,1536]{1,0:T(8,128)(2,1)}), bf16[1024,1536]{1,0:T(8,128)(2,1)}) %all-gather.9.cloned.1.call-update) | async-done | bytes 3145744 | tf_op jit(solution)/shard_map/all_gather | solution.py:76
  137.0 4.5 fusion.41
  141.6 1.5 multiply_convert_fusion.6
  143.1 3.7 fusion.42
  147.5 130.2 %reduce-scatter.13.cloned.1.call-done = f32[128,1536]{1,0:T(8,128)} async-done(((f32[1024,1536]{1,0:T(8,128)}), f32[128,1536]{1,0:T(8,128)}) %reduce-scatter.13.cloned.1.call-update) | async-done | bytes 786448 | tf_op jit(solution)/shard_map/reduce_scatter | solution.py:88
  283.1 1.9 fusion.30
  285.2 44.4 %all-gather.15.cloned.1.call-done = bf16[1536,864]{1,0:T(8,128)(2,1)} async-done(((bf16[96,864]{1,0:T(8,128)(2,1)}), bf16[1536,864]{1,0:T(8,128)(2,1)}) %all-gather.15.cloned.1.call-update) | async-done | bytes 2654224 | tf_op jit(solution)/shard_map/all_gather | solution.py:62
  329.6 73.2 %all-gather.13.cloned.1.call-done = bf16[1024,1536]{1,0:T(8,128)(2,1)} async-done(((bf16[128,1536]{1,0:T(8,128)(2,1)}), bf16[1024,1536]{1,0:T(8,128)(2,1)}) %all-gather.13.cloned.1.call-update) | async-done | bytes 3145744 | tf_op jit(solution)/shard_map/all_gather | solution.py:95
  402.8 7.5 fusion.43
  410.3 44.4 %all-gather.17.cloned.1.call-done = bf16[1536,864]{1,0:T(8,128)(2,1)} async-done(((bf16[96,864]{1,0:T(8,128)(2,1)}), bf16[1536,864]{1,0:T(8,128)(2,1)}) %all-gather.17.cloned.1.call-update) | async-done | bytes 2654224 | tf_op jit(solution)/shard_map/all_gather | solution.py:63
  454.7 7.5 fusion.44
  462.3 44.5 %all-gather.19.cloned.1.call-done = bf16[864,1536]{0,1:T(8,128)(2,1)} async-done(((bf16[864,96]{0,1:T(8,128)(2,1)}), bf16[864,1536]{0,1:T(8,128)(2,1)}) %all-gather.19.cloned.1.call-update) | async-done | bytes 2654224 | tf_op jit(solution)/shard_map/all_gather | solution.py:65
  506.8 73.3 %all-gather.21.cloned.1.call-done = bf16[1024,1536]{1,0:T(8,128)(2,1)} async-done(((bf16[128,1536]{1,0:T(8,128)(2,1)}), bf16[1024,1536]{1,0:T(8,128)(2,1)}) %all-gather.21.cloned.1.call-update) | async-done | bytes 3145744 | tf_op jit(solution)/shard_map/all_gather | solution.py:117
  580.1 10.5 multiply_convert_fusion
  590.7 3.7 fusion.45
  594.5 5.0 add_convert_fusion
  599.6 71.6 %reduce-scatter.17.cloned.1.call-done = bf16[128,1536]{1,0:T(8,128)(2,1)} async-done(((bf16[1024,1536]{1,0:T(8,128)(2,1)}), bf16[128,1536]{1,0:T(8,128)(2,1)}) %reduce-scatter.17.cloned.1.call-update) | async-done | bytes 393232 | tf_op jit(solution)/shard_map/reduce_scatter | solution.py:138
  671.2 1.9 fusion.23
  673.7 2.2 fusion.37
  675.9 7.4 convolution_convert_fusion.3
  683.4 7.5 convolution_convert_fusion.2
  691.4 7.4 convolution_convert_fusion.1
  698.9 48.2 %all-gather.23.cloned.1.call-done = bf16[1024,1536]{1,0:T(8,128)(2,1)} async-done(((bf16[128,1536]{1,0:T(8,128)(2,1)}), bf16[1024,1536]{1,0:T(8,128)(2,1)}) %all-gather.23.cloned.1.call-update) | async-done | bytes 3145744 | tf_op jit(solution)/shard_map/all_gather | solution.py:145
  747.1 3.6 convolution_convert_fusion.5
  750.7 2.2 copy.33
  753.1 5.0 multiply_reduce_fusion.1
  760.6 3.9 convolution_convert_fusion.4
  764.6 5.4 bitcast_convert_fusion
  771.5 6.8 convolution_convert_fusion
  778.4 45.2 %reduce-scatter.23.cloned.1.call-done = bf16[96,864]{1,0:T(8,128)(2,1)} async-done(((bf16[1536,864]{1,0:T(8,128)(2,1)}), bf16[96,864]{1,0:T(8,128)(2,1)}) %reduce-scatter.23.cloned.1.call-update) | async-done | bytes 165904 | tf_op jit(solution)/shard_map/reduce_scatter | solution.py:149
  823.6 1.7 convert_element_type.138
  825.3 75.0 %reduce-scatter.25.cloned.1.call-done = bf16[96,864]{1,0:T(8,128)(2,1)} async-done(((bf16[1536,864]{1,0:T(8,128)(2,1)}), bf16[96,864]{1,0:T(8,128)(2,1)}) %reduce-scatter.25.cloned.1.call-update) | async-done | bytes 165904 | tf_op jit(solution)/shard_map/reduce_scatter | solution.py:152
  900.2 1.7 convert_element_type.140
  901.9 75.1 %reduce-scatter.27.cloned.1.call-done = bf16[864,96]{0,1:T(8,128)(2,1)} async-done(((bf16[864,1536]{0,1:T(8,128)(2,1)}), bf16[864,96]{0,1:T(8,128)(2,1)}) %reduce-scatter.27.cloned.1.call-update) | async-done | bytes 165904 | tf_op jit(solution)/shard_map/reduce_scatter | solution.py:155
  977.0 1.7 convert_element_type.142
  979.0 66.4 %reduce-scatter.29.cloned.1.call-done = bf16[96,192]{1,0:T(8,128)(2,1)} async-done(((bf16[1536,192]{1,0:T(8,128)(2,1)}), bf16[96,192]{1,0:T(8,128)(2,1)}) %reduce-scatter.29.cloned.1.call-update) | async-done | bytes 36880
  1047.0 73.6 %reduce-scatter.21.cloned.1.call-done = bf16[96,3,192]{2,0,1:T(8,128)(2,1)} async-done(((bf16[1536,3,192]{2,0,1:T(8,128)(2,1)}), bf16[96,3,192]{2,0,1:T(8,128)(2,1)}) %reduce-scatter.21.cloned.1.call-update) | async-done | bytes 110608 | tf_op jit(solution)/shard_map/reduce_scatter | solution.py:201
  1120.6 1.6 convert_element_type.134
  1122.3 72.5 %reduce-scatter.19.cloned.1.call-done = bf16[128,1536]{1,0:T(8,128)(2,1)} async-done(((bf16[1024,1536]{1,0:T(8,128)(2,1)}), bf16[128,1536]{1,0:T(8,128)(2,1)}) %reduce-scatter.19.cloned.1.call-update) | async-done | bytes 393232 | tf_op jit(solution)/shard_map/reduce_scatter | solution.py:187
  1196.1 65.7 %all-reduce.9 = (f32[1536]{0:T(1024)S(1)}, f32[3,1536]{1,0:T(4,128)S(1)}, f32[1536]{0:T(1024)S(1)}) all-reduce(f32[1536]{0:T(1024)S(1)} %get-tuple-element.14, f32[3,1536]{1,0:T(4,128)S(1)} %dynamic_update_slice.3, f32[1536]{0:T(1024)S(1)} %copy-done.10), channel_id=6, replica_groups=mesh['dp'=16,'tensor'=8] {'dp','tensor'}, use_global_device_ids=true, to_apply=%region_9.10.clone | all-reduce | flops 7680 | bytes 61440
  1263.6 6.7 reduce-scatter.15.cloned.1.call-done
  1270.4 2.6 fusion.19
  (133 shorter events, 21.3 us)
Async XLA Ops:
  7.2 71.1 %all-gather.11.cloned.1.call-start = ((), (), s32[]{:S(2)}) async-start(), calls=%async_computation.10 | async-start | bytes 3342336 | tf_op jit(solution)/shard_map/all_gather | solution.py:57
  9.0 128.0 %all-gather.9.cloned.1.call-start = ((), (), s32[]{:S(2)}) async-start(), calls=%async_computation.9 | async-start | bytes 3538944 | tf_op jit(solution)/shard_map/all_gather | solution.py:76
  45.1 1.9 copy-start.19
  47.0 230.7 %reduce-scatter.13.cloned.1.call-start = ((), (), s32[]{:S(2)}) async-start(), calls=%async_computation.11 | async-start | bytes 7077888 | tf_op jit(solution)/shard_map/reduce_scatter | solution.py:88
  49.3 92.2 %copy-start.11 = (f32[1,192]{1,0:T(1,128)}, f32[1,192]{1,0:T(1,128)S(1)}, u32[]{:S(2)}) copy-start(f32[1,192]{1,0:T(1,128)S(1)} %get-tuple-element.35) | copy-start | bytes 2308
  49.4 92.2 %copy-start.13 = (f32[1,192]{1,0:T(1,128)}, f32[1,192]{1,0:T(1,128)S(1)}, u32[]{:S(2)}) copy-start(f32[1,192]{1,0:T(1,128)S(1)} %get-tuple-element.36) | copy-start | bytes 2308
  137.0 4.6 copy-start.15
  141.5 5.3 copy-start.1
  141.6 1.6 copy-start.2
  143.1 3.7 copy-start.3
  146.8 130.9 %copy-start = (bf16[128,1536]{1,0:T(8,128)(2,1)S(1)}, bf16[128,1536]{1,0:T(8,128)(2,1)}, u32[]{:S(2)}) copy-start(bf16[128,1536]{1,0:T(8,128)(2,1)} %param.11) | copy-start | bytes 1179652
  146.8 182.8 %all-gather.15.cloned.1.call-start = ((), (), s32[]{:S(2)}) async-start(), calls=%async_computation.13 | async-start | bytes 2924544 | tf_op jit(solution)/shard_map/all_gather | solution.py:62
  147.4 255.4 %all-gather.13.cloned.1.call-start = ((), (), s32[]{:S(2)}) async-start(), calls=%async_computation.12 | async-start | bytes 3538944 | tf_op jit(solution)/shard_map/all_gather | solution.py:95
  280.5 174.2 %all-gather.17.cloned.1.call-start = ((), (), s32[]{:S(2)}) async-start(), calls=%async_computation.14 | async-start | bytes 2924544 | tf_op jit(solution)/shard_map/all_gather | solution.py:63
  281.1 225.7 %all-gather.19.cloned.1.call-start = ((), (), s32[]{:S(2)}) async-start(), calls=%async_computation.15 | async-start | bytes 2924544 | tf_op jit(solution)/shard_map/all_gather | solution.py:65
  281.9 298.3 %all-gather.21.cloned.1.call-start = ((), (), s32[]{:S(2)}) async-start(), calls=%async_computation.17 | async-start | bytes 3538944 | tf_op jit(solution)/shard_map/all_gather | solution.py:117
  285.0 386.2 %reduce-scatter.17.cloned.1.call-start = ((), (), s32[]{:S(2)}) async-start(), calls=%async_computation.18 | async-start | bytes 3538944 | tf_op jit(solution)/shard_map/reduce_scatter | solution.py:138
  580.1 10.5 copy-start.30
  590.7 3.7 copy-start.32
  590.7 3.8 copy-start.34
  590.7 3.8 copy-start.31
  599.5 147.6 %all-gather.23.cloned.1.call-start = ((), (), s32[]{:S(2)}) async-start(), calls=%async_computation.19 | async-start | bytes 3538944 | tf_op jit(solution)/shard_map/all_gather | solution.py:145
  675.9 147.7 %reduce-scatter.23.cloned.1.call-start = ((), (), s32[]{:S(2)}) async-start(), calls=%async_computation.22 | async-start | bytes 2924544 | tf_op jit(solution)/shard_map/reduce_scatter | solution.py:149
  683.4 216.9 %reduce-scatter.25.cloned.1.call-start = ((), (), s32[]{:S(2)}) async-start(), calls=%async_computation.23 | async-start | bytes 2924544 | tf_op jit(solution)/shard_map/reduce_scatter | solution.py:152
  690.9 286.1 %reduce-scatter.27.cloned.1.call-start = ((), (), s32[]{:S(2)}) async-start(), calls=%async_computation.24 | async-start | bytes 2924544 | tf_op jit(solution)/shard_map/reduce_scatter | solution.py:155
  698.8 346.6 %reduce-scatter.29.cloned.1.call-start = ((), (), s32[]{:S(2)}) async-start(), calls=%async_computation.25 | async-start | bytes 835584
  753.0 367.6 %reduce-scatter.21.cloned.1.call-start = ((), (), s32[]{:S(2)}) async-start(), calls=%async_computation.21 | async-start | bytes 2506752 | tf_op jit(solution)/shard_map/reduce_scatter | solution.py:201
  753.1 5.1 copy-start.12
  753.1 5.1 copy-start.14
  753.1 5.1 copy-start.16
  758.1 0.8 copy-start.7
  758.2 2.4 copy-start.29
  758.8 0.8 copy-start.8
  758.9 0.7 copy-start.9
  760.6 4.0 copy-start.6
  764.5 430.3 %reduce-scatter.19.cloned.1.call-start = ((), (), s32[]{:S(2)}) async-start(), calls=%async_computation.20 | async-start | bytes 3538944 | tf_op jit(solution)/shard_map/reduce_scatter | solution.py:187
  770.0 1.5 copy-start.33
  770.0 500.4 %reduce-scatter.15.cloned.1.call-start = ((), (), s32[]{:S(2)}) async-start(), calls=%async_computation.16 | async-start | bytes 3538944 | tf_op jit(solution)/shard_map/reduce_scatter | solution.py:102
  778.3 200.4 %copy-start.23 = (f32[192]{0:T(256)S(1)}, f32[192]{0:T(256)}, u32[]{:S(2)}) copy-start(f32[192]{0:T(256)} %get-tuple-element.10) | copy-start | bytes 2308
  778.3 200.4 %copy-start.24 = (f32[192]{0:T(256)S(1)}, f32[192]{0:T(256)}, u32[]{:S(2)}) copy-start(f32[192]{0:T(256)} %get-tuple-element.11) | copy-start | bytes 2308
  778.3 200.4 %copy-start.25 = (f32[192]{0:T(256)S(1)}, f32[192]{0:T(256)}, u32[]{:S(2)}) copy-start(f32[192]{0:T(256)} %get-tuple-element.16) | copy-start | bytes 2308
  778.3 416.5 %copy-start.20 = (f32[128]{0:T(128)S(1)}, f32[128]{0:T(128)}, u32[]{:S(2)}) copy-start(f32[128]{0:T(128)} %copy-done.19) | copy-start | bytes 1540
  778.3 417.8 %copy-start.10 = (f32[1536]{0:T(1024)S(1)}, f32[1536]{0:T(1024)}, u32[]{:S(2)}) copy-start(f32[1536]{0:T(1024)} %get-tuple-element.12) | copy-start | bytes 18436
  778.3 492.0 %copy-start.4 = (bf16[128,1536]{1,0:T(8,128)(2,1)S(1)}, bf16[128,1536]{1,0:T(8,128)(2,1)}, u32[]{:S(2)}) copy-start(bf16[128,1536]{1,0:T(8,128)(2,1)} %param.21) | copy-start | bytes 1179652
  778.3 492.0 %copy-start.5 = (bf16[128,1536]{1,0:T(8,128)(2,1)S(1)}, bf16[128,1536]{1,0:T(8,128)(2,1)}, u32[]{:S(2)}) copy-start(bf16[128,1536]{1,0:T(8,128)(2,1)} %reduce-scatter.17.cloned.1.call-done) | copy-start | bytes 1179652
  778.4 492.0 %copy-start.18 = (f32[128]{0:T(128)S(1)}, f32[128]{0:T(128)}, u32[]{:S(2)}) copy-start(f32[128]{0:T(128)} %copy-done.17) | copy-start | bytes 1540
  778.4 492.0 %copy-start.22 = (f32[128]{0:T(128)S(1)}, f32[128]{0:T(128)}, u32[]{:S(2)}) copy-start(f32[128]{0:T(128)} %copy-done.21) | copy-start | bytes 1540
  778.4 492.0 %copy-start.28 = (f32[128]{0:T(128)S(1)}, f32[128]{0:T(128)}, u32[]{:S(2)}) copy-start(f32[128]{0:T(128)} %copy-done.27) | copy-start | bytes 1540
  (4 other events, 2.4 us)
Sparse Core Ops, SparseCore 0:
  11.0 52.7 all-gather.10
  66.0 70.9 all-gather.8
  147.0 130.7 reduce-scatter.12
  280.0 49.6 all-gather.14
  331.7 71.0 all-gather.12
  405.1 49.6 all-gather.16
  457.1 49.6 all-gather.18
  509.0 71.0 all-gather.20
  599.6 71.5 reduce-scatter.16
  676.0 71.0 all-gather.22
  751.1 72.4 reduce-scatter.22
  827.4 72.7 reduce-scatter.24
  904.2 72.7 reduce-scatter.26
  980.6 64.8 reduce-scatter.28
  1049.3 71.2 reduce-scatter.20
  1122.9 71.8 reduce-scatter.18
  1197.0 73.2 reduce-scatter.14
where the time goes:
time: 1290 us; the launch traced here: 1280 us
  waiting for transfers between devices  1000 us (78%)
  blocking collectives  126 us (10%)
  matrix products  89.6 us (7%)
  other arithmetic  24.8 us (2%)
  local copies, waits for them, and re-layouts  22.5 us (2%)
  between operations  15.9 us (1%)
    reduce_scatter x1, waiting for transfers between devices, per_device(): lax.psum_scatter(mixer_part, 'tensor', scatter_dimension=0, tiled=True)  130 us
    unnamed x2, blocking collectives  97 us
    reduce_scatter x1, waiting for transfers between devices, per_device(): lax.psum_scatter(down_full.astype(jnp.bfloat16), 'dp', scatter_dimension=...  75.1 us
    reduce_scatter x1, waiting for transfers between devices, per_device(): lax.psum_scatter(up_full.astype(jnp.bfloat16), 'dp', scatter_dimension=0,...  75 us
    reduce_scatter x1, waiting for transfers between devices, per_device(): lax.psum_scatter(in_full.astype(jnp.bfloat16), 'dp', scatter_dimension=0,...  73.6 us
    all_gather x1, waiting for transfers between devices, per_device(): lax.all_gather(output_gradient.astype(jnp.bfloat16), 'tensor', axis=0, ti...  73.3 us
    all_gather x1, waiting for transfers between devices, per_device(): lax.all_gather(second_normalized_rows, 'tensor', axis=0, tiled=True)  73.2 us
    reduce_scatter x1, waiting for transfers between devices, per_device(): lax.psum_scatter(gradient_of_normalized.astype(jnp.bfloat16), 'tensor', s...  72.5 us
  transfers between devices with their start and end apart: 17, of which 16 were waited for; matrix products, arithmetic and copies ran while one was open for 7% of the time, Pallas kernels for 0%

commit v1 on v0

v1 whole, which is shorter than its diff:
```python
import functools

import jax
import jax.numpy as jnp
from jax import lax
from jax.experimental import pallas as pl
from jax.experimental.pallas import tpu as pltpu
from jax.sharding import PartitionSpec as P

epsilon = 1e-05
MESH = pl.DeviceIdType.MESH
BF = jnp.bfloat16
F32 = jnp.float32
D = 1536
ROWS = 128
CH = 192
FB = 864
FP = 896
HALF = 48
VMEM_LIMIT = 60 << 20


class Place:
    def __init__(self):
        dp = lax.axis_index("dp")
        t = lax.axis_index("tensor")
        self.x, self.yh, self.c = dp // 4, (dp // 2) % 2, dp % 2
        self.z, self.yl = t // 2, t % 2
        self.y = self.yh * 2 + self.yl
        self.o = 1 - self.c
        self.xp, self.xm, self.x2 = (self.x + 1) % 4, (self.x + 3) % 4, (self.x + 2) % 4
        self.yp, self.ym = (self.y + 1) % 4, (self.y + 3) % 4
        self.yhp, self.yhm = self.yp // 2, self.ym // 2
        self.way = 1 - 2 * self.c
        self.zf = (self.z + self.way + 4) % 4
        self.zb = (self.z - self.way + 4) % 4
        self.zp, self.zm, self.z2 = (self.z + 1) % 4, (self.z + 3) % 4, (self.z + 2) % 4
        self.own = self.c == self.yl
        self.opp = self.c != self.yl

    def at(self, x=None, y=None, z=None, c=None):
        x = self.x if x is None else x
        y = self.y if y is None else y
        z = self.z if z is None else z
        c = self.c if c is None else c
        return (x * 4 + (y // 2) * 2 + c, z * 2 + y % 2)


class Net:
    def __init__(self, place, send, recv, local=None):
        self.p, self.ss, self.rs, self.ls = place, send, recv, local
        self.ns = self.nr = self.nl = 0
        self.pending = []

    def sem(self, n=1):
        k = self.nr
        self.nr += n
        return k

    def send(self, src, dst, recv_index, target, cond=None):
        k = self.ns
        self.ns += 1
        d = pltpu.make_async_remote_copy(
            src_ref=src, dst_ref=dst, send_sem=self.ss.at[k], recv_sem=self.rs.at[recv_index],
            device_id=target, device_id_type=MESH)
        run(cond, d.start)
        self.pending.append((cond, d))

    def copy(self, src, dst, cond=None):
        k = self.nl
        self.nl += 1
        d = pltpu.make_async_copy(src, dst, self.ls.at[k])
        run(cond, d.start)
        return lambda: run(cond, d.wait)

    def got(self, dst, recv_index, cond=None):
        d = pltpu.make_async_remote_copy(
            src_ref=dst, dst_ref=dst, send_sem=self.ss.at[0], recv_sem=self.rs.at[recv_index],
            device_id=self.p.at(c=self.p.o), device_id_type=MESH)
        run(cond, d.wait_recv)

    def finish(self):
        for cond, d in self.pending:
            run(cond, d.wait_send)
        self.pending = []


def run(cond, f):
    if cond is None:
        f()
    else:
        pl.when(cond)(f)


def greet(p, plane, ring):
    bar = pltpu.get_barrier_semaphore()
    who = [p.at(c=p.o)]
    if plane:
        for c in (0, 1):
            who += [p.at(x=p.xp, c=c), p.at(x=p.xm, c=c), p.at(y=p.yp, c=c), p.at(y=p.ym, c=c)]
    if ring:
        who += [p.at(z=p.zp), p.at(z=p.zm)]
    for w in who:
        pl.semaphore_signal(bar, inc=1, device_id=w, device_id_type=MESH)
    pl.semaphore_wait(bar, len(who))


def together(*jobs):
    jobs = list(jobs)
    while jobs:
        for j in list(jobs):
            try:
                next(j)
            except StopIteration:
                jobs.remove(j)


HA, HB = pl.ds(0, HALF), pl.ds(HALF, HALF)


def gather_plane(net, sh, W):
    p = net.p
    i_own, f1, f2, f3, f4 = net.sem(), net.sem(2), net.sem(2), net.sem(2), net.sem(2)
    r1, r2, r3, r4, y1, y2, y3, y4, x1, x2, x3, x4 = (net.sem() for _ in range(12))
    q = p.yl
    done = net.copy(sh, W.at[p.x, p.yh, p.c], p.own)
    net.send(sh.at[HA], W.at[p.x, p.yh, p.c, HA], f1 + p.c, p.at(x=p.xp, c=q))
    net.send(sh.at[HA], W.at[p.x, p.yh, p.c, HA], f2 + p.c, p.at(x=p.xm, c=q))
    net.send(sh.at[HB], W.at[p.x, p.yh, p.c, HB], f3 + p.c, p.at(y=p.yp, c=q))
    net.send(sh.at[HB], W.at[p.x, p.yh, p.c, HB], f4 + p.c, p.at(y=p.ym, c=q))
    net.send(sh, W.at[p.x, p.yh, p.c], i_own, p.at(c=p.o), p.opp)
    yield
    net.got(W.at[p.xm, p.yh, 0, HA], f1 + 0, p.own)
    net.got(W.at[p.x, p.yhm, 0, HB], f3 + 0, p.opp)
    net.send(W.at[p.xm, p.yh, 0, HA], W.at[p.xm, p.yh, 0, HA], r1, p.at(x=p.xp), p.own)
    net.send(W.at[p.x, p.yhm, 0, HB], W.at[p.x, p.yhm, 0, HB], r3, p.at(y=p.yp), p.opp)
    net.got(W.at[p.xp, p.yh, 1, HA], f2 + 1, p.own)
    net.got(W.at[p.x, p.yhp, 1, HB], f4 + 1, p.opp)
    net.send(W.at[p.xp, p.yh, 1, HA], W.at[p.xp, p.yh, 1, HA], r2, p.at(x=p.xm), p.own)
    net.send(W.at[p.x, p.yhp, 1, HB], W.at[p.x, p.yhp, 1, HB], r4, p.at(y=p.ym), p.opp)
    yield
    done()
    net.got(W.at[p.x, p.yh, p.o], i_own, p.own)
    net.got(W.at[p.xm, p.yh, 1, HA], f1 + 1, p.own)
    net.got(W.at[p.xp, p.yh, 0, HA], f2 + 0, p.own)
    net.got(W.at[p.x, p.yhm, 1, HB], f3 + 1, p.opp)
    net.got(W.at[p.x, p.yhp, 0, HB], f4 + 0, p.opp)
    net.got(W.at[p.x2, p.yh, 0, HA], r1, p.own)
    net.got(W.at[p.x2, p.yh, 1, HA], r2, p.own)
    net.send(W.at[:, p.yh, :, HA], W.at[:, p.yh, :, HA], y1, p.at(y=p.yp), p.own)
    net.send(W.at[:, p.yh, :, HA], W.at[:, p.yh, :, HA], y2, p.at(y=p.ym), p.own)
    net.got(W.at[p.x, 1 - p.yh, 0, HB], r3, p.own)
    net.got(W.at[p.x, 1 - p.yh, 1, HB], r4, p.own)
    net.send(W.at[p.x, :, :, HB], W.at[p.x, :, :, HB], x1, p.at(x=p.xp))
    net.send(W.at[p.x, :, :, HB], W.at[p.x, :, :, HB], x2, p.at(x=p.xm))
    yield
    net.got(W.at[:, p.yhm, :, HA], y1, p.opp)
    net.send(W.at[:, p.yhm, 0, HA], W.at[:, p.yhm, 0, HA], y3, p.at(y=p.yp), p.opp)
    net.got(W.at[:, p.yhp, :, HA], y2, p.opp)
    net.send(W.at[:, p.yhp, 1, HA], W.at[:, p.yhp, 1, HA], y4, p.at(y=p.ym), p.opp)
    net.got(W.at[p.xm, :, :, HB], x1)
    net.send(W.at[p.xm, :, 0, HB], W.at[p.xm, :, 0, HB], x3, p.at(x=p.xp))
    net.got(W.at[p.xp, :, :, HB], x2)
    net.send(W.at[p.xp, :, 1, HB], W.at[p.xp, :, 1, HB], x4, p.at(x=p.xm))
    yield
    net.got(W.at[:, 1 - p.yh, 0, HA], y3, p.own)
    net.got(W.at[:, 1 - p.yh, 1, HA], y4, p.own)
    net.got(W.at[p.x2, :, 0, HB], x3)
    net.got(W.at[p.x2, :, 1, HB], x4)


def add(out, *terms):
    lead = out.shape[:-2]
    count = 1
    for s in lead:
        count *= s

    def one(i):
        at = []
        for s in reversed(lead):
            at.append(i % s)
            i = i // s
        at = tuple(reversed(at))
        v = terms[0][at].astype(F32) if at else terms[0][...].astype(F32)
        for t in terms[1:]:
            v = v + (t[at] if at else t[...]).astype(F32)
        if at:
            out[at] = v.astype(out.dtype)
        else:
            out[...] = v.astype(out.dtype)

    if count == 1 and not lead:
        one(0)
    else:
        lax.fori_loop(0, count, lambda i, _: one(i), None)


def plane_scratch(n):
    return [
        pltpu.VMEM((2, 4, HALF, n), BF),
        pltpu.VMEM((2, 4, 2, HALF, n), BF),
        pltpu.VMEM((2, HALF, n), BF),
        pltpu.VMEM((3, HALF, n), BF),
        pltpu.VMEM((2, 2, HALF, n), BF),
        pltpu.VMEM((2, 2, 2, HALF, n), BF),
        pltpu.VMEM((2, HALF, n), BF),
        pltpu.VMEM((3, HALF, n), BF),
    ]


def reduce_plane(net, G, out, RA, RB, RC, F, RX, RY, RZ, H):
    p = net.p
    a0, a1, bp0, bp1, bm0, bm1, c0, c1, g0, g1, g2 = (net.sem() for _ in range(11))
    u0, u1, vp0, vp1, vm0, vm1, w0, w1, h0, h1, h2 = (net.sem() for _ in range(11))
    net.send(G.at[:, 1 - p.yh, 0, HA], RA.at[0], a0, p.at(y=p.ym), p.own)
    net.send(G.at[:, 1 - p.yh, 1, HA], RA.at[1], a1, p.at(y=p.yp), p.own)
    net.send(G.at[p.x2, :, 0, HB], RX.at[0], u0, p.at(x=p.xm))
    net.send(G.at[p.x2, :, 1, HB], RX.at[1], u1, p.at(x=p.xp))
    net.send(G.at[:, p.yhm, 1, HA], RB.at[0, :, 1], bp1, p.at(y=p.ym), p.opp)
    net.send(G.at[:, p.yhp, 0, HA], RB.at[1, :, 0], bm0, p.at(y=p.yp), p.opp)
    net.send(G.at[p.xm, :, 1, HB], RY.at[0, :, 1], vp1, p.at(x=p.xm))
    net.send(G.at[p.xp, :, 0, HB], RY.at[1, :, 0], vm0, p.at(x=p.xp))
    yield

    net.got(RA.at[0], a0, p.opp)
    net.got(RA.at[1], a1, p.opp)

    @pl.when(p.opp)
    def _():
        add(RA.at[0], RA.at[0], G.at[:, p.yhm, 0, HA])
        add(RA.at[1], RA.at[1], G.at[:, p.yhp, 1, HA])

    net.send(RA.at[0], RB.at[0, :, 0], bp0, p.at(y=p.ym), p.opp)
    net.send(RA.at[1], RB.at[1, :, 1], bm1, p.at(y=p.yp), p.opp)
    net.got(RX.at[0], u0)
    add(RX.at[0], RX.at[0], G.at[p.xm, :, 0, HB])
    net.send(RX.at[0], RY.at[0, :, 0], vp0, p.at(x=p.xm))
    net.got(RX.at[1], u1)
    add(RX.at[1], RX.at[1], G.at[p.xp, :, 1, HB])
    net.send(RX.at[1], RY.at[1, :, 1], vm1, p.at(x=p.xp))
    yield

    net.got(RB.at[0, :, 1], bp1, p.own)
    net.got(RB.at[1, :, 0], bm0, p.own)
    net.got(RB.at[0, :, 0], bp0, p.own)
    net.got(RB.at[1, :, 1], bm1, p.own)

    @pl.when(p.own)
    def _():
        add(RB.at[0], RB.at[0], RB.at[1], G.at[:, p.yh, :, HA])

    S = RB.at[0]
    net.send(S.at[p.x2, 0], RC.at[0], c0, p.at(x=p.xm), p.own)
    net.send(S.at[p.x2, 1], RC.at[1], c1, p.at(x=p.xp), p.own)
    net.send(S.at[p.xm, 1], F.at[1], g1, p.at(x=p.xm, c=1), p.own)
    net.send(S.at[p.xp, 0], F.at[2], g2, p.at(x=p.xp, c=0), p.own)
    net.send(S.at[p.x, p.o], F.at[0], g0, p.at(c=p.o), p.own)

    net.got(RY.at[0, :, 1], vp1)
    net.got(RY.at[1, :, 0], vm0)
    net.got(RY.at[0, :, 0], vp0)
    net.got(RY.at[1, :, 1], vm1)
    add(RY.at[0], RY.at[0], RY.at[1], G.at[p.x, :, :, HB])
    T = RY.at[0]
    net.send(T.at[1 - p.yh, 0], RZ.at[0], w0, p.at(y=p.ym), p.own)
    net.send(T.at[1 - p.yh, 1], RZ.at[1], w1, p.at(y=p.yp), p.own)
    net.send(T.at[p.yhm, 1], H.at[1], h1, p.at(y=p.ym, c=1), p.opp)
    net.send(T.at[p.yhp, 0], H.at[2], h2, p.at(y=p.yp, c=0), p.opp)
    net.send(T.at[p.yh, p.o], H.at[0], h0, p.at(c=p.o), p.own)
    yield

    net.got(RC.at[0], c0, p.own)
    net.got(RC.at[1], c1, p.own)
    net.got(RZ.at[0], w0, p.opp)
    net.got(RZ.at[1], w1, p.opp)

    @pl.when(p.own)
    def _():
        add(RC.at[0], RC.at[0], S.at[p.xm, 0])
        add(RC.at[1], RC.at[1], S.at[p.xp, 1])

    @pl.when(p.opp)
    def _():
        add(RZ.at[0], RZ.at[0], T.at[p.yhm, 0])
        add(RZ.at[1], RZ.at[1], T.at[p.yhp, 1])

    net.send(RC.at[0], F.at[1], g1, p.at(x=p.xm, c=0), p.own)
    net.send(RC.at[1], F.at[2], g2, p.at(x=p.xp, c=1), p.own)
    net.send(RZ.at[0], H.at[1], h1, p.at(y=p.ym, c=0), p.opp)
    net.send(RZ.at[1], H.at[2], h2, p.at(y=p.yp, c=1), p.opp)
    yield

    net.got(F.at[0], g0, p.opp)
    net.got(F.at[1], g1)
    net.got(F.at[2], g2)
    net.got(H.at[0], h0, p.opp)
    net.got(H.at[1], h1)
    net.got(H.at[2], h2)

    @pl.when(p.own)
    def _():
        F[0] = S[p.x, p.c]
        H[0] = T[p.yh, p.c]

    add(out.at[HA], F.at[0], F.at[1], F.at[2])
    add(out.at[HB], H.at[0], H.at[1], H.at[2])


def gather_ring(net, a, out):
    p = net.p
    s1, s3, s2 = net.sem(), net.sem(), net.sem()
    k = net.sem(4)
    done = net.copy(a, out.at[p.c, p.z])
    net.send(a, out.at[p.c, p.z], s1, p.at(z=p.zf))
    net.send(a, out.at[p.c, p.z], s3, p.at(z=p.zb))
    net.send(a, out.at[p.c, p.z], k + 0, p.at(c=p.o))
    yield
    net.got(out.at[p.c, p.zb], s1)
    net.send(out.at[p.c, p.zb], out.at[p.c, p.zb], s2, p.at(z=p.zf))
    net.send(out.at[p.c, p.zb], out.at[p.c, p.zb], k + (p.zb - p.z + 4) % 4, p.at(c=p.o))
    net.got(out.at[p.c, p.zf], s3)
    net.send(out.at[p.c, p.zf], out.at[p.c, p.zf], k + (p.zf - p.z + 4) % 4, p.at(c=p.o))
    yield
    net.got(out.at[p.c, p.z2], s2)
    net.send(out.at[p.c, p.z2], out.at[p.c, p.z2], k + 2, p.at(c=p.o))
    yield
    done()
    for j in range(4):
        net.got(out.at[p.o, (p.z + j) % 4], k + j)


def ring_scratch(n):
    return [pltpu.VMEM((4, ROWS, n), BF), pltpu.VMEM((2, ROWS, n), BF), pltpu.VMEM((3, ROWS, n), BF)]


def reduce_ring(net, V, out, RC, SB, RZ):
    p = net.p
    s2, sd, sr = net.sem(), net.sem(), net.sem()
    k = net.sem(4)
    for j in (2, 1, 3, 0):
        zj = (p.z + j) % 4
        net.send(V.at[p.o, zj], RC.at[j], k + j, p.at(c=p.o))
    yield
    jf, jb = (p.zf - p.z + 4) % 4, (p.zb - p.z + 4) % 4
    net.got(RC.at[2], k + 2)
    add(SB.at[0], V.at[p.c, p.z2], RC.at[2])
    net.send(SB.at[0], RZ.at[0], s2, p.at(z=p.zf))
    net.got(RC.at[jb], k + jb)
    add(SB.at[1], V.at[p.c, p.zb], RC.at[jb])
    net.send(SB.at[1], RZ.at[1], sd, p.at(z=p.zb))
    net.got(RC.at[jf], k + jf)
    add(RC.at[jf], V.at[p.c, p.zf], RC.at[jf])
    yield
    net.got(RZ.at[0], s2)
    add(RC.at[jf], RC.at[jf], RZ.at[0])
    net.send(RC.at[jf], RZ.at[2], sr, p.at(z=p.zf))
    net.got(RC.at[0], k + 0)
    add(RC.at[0], V.at[p.c, p.z], RC.at[0])
    yield
    net.got(RZ.at[1], sd)
    net.got(RZ.at[2], sr)
    add(out, RC.at[0], RZ.at[1], RZ.at[2])


def shape(s, t=BF):
    return jax.ShapeDtypeStruct(s, t)


def slots(n):
    return shape((4, 2, 2, 96, n))


def blocks(n):
    return shape((2, 4, ROWS, n))


def exchange(name, number, gathers=(), rings=(), ring_sums=(), plane_sums=()):
    ng, nz, ns, nq = len(gathers), len(rings), len(ring_sums), len(plane_sums)

    def kernel(*refs):
        refs = list(refs)

        def take(n):
            part, refs[:] = refs[:n], refs[n:]
            return part

        a, b, d, e = take(ng), take(nz), take(ns), take(nq)
        ao, bo, do, eo = take(ng), take(nz), take(ns), take(nq)
        ds = [take(3) for _ in range(ns)]
        es = [take(8) for _ in range(nq)]
        send, recv, local = refs
        p = Place()
        greet(p, bool(ng + nq), bool(nz + ns))
        net = Net(p, send, recv, local)
        jobs = [reduce_ring(net, v, o, *s) for v, o, s in zip(d, do, ds)]
        jobs += [gather_ring(net, v, o) for v, o in zip(b, bo)]
        jobs += [gather_plane(net, v, o) for v, o in zip(a, ao)]
        jobs += [reduce_plane(net, v, o, *s) for v, o, s in zip(e, eo, es)]
        together(*jobs)
        net.finish()

    any_, vm = pl.BlockSpec(memory_space=pl.ANY), pl.BlockSpec(memory_space=pltpu.VMEM)
    scratch = []
    for v in ring_sums:
        scratch += ring_scratch(v.shape[-1])
    for v in plane_sums:
        scratch += plane_scratch(v.shape[-1])
    count = 24 * (ng + nq) + 12 * (nz + ns)
    scratch += [pltpu.SemaphoreType.DMA((count,))] * 2 + [pltpu.SemaphoreType.DMA((ng + nz + 1,))]
    outs = [slots(v.shape[-1]) for v in gathers] + [blocks(v.shape[-1]) for v in rings]
    outs += [shape((ROWS, v.shape[-1]), F32) for v in ring_sums]
    outs += [shape((96, v.shape[-1]), F32) for v in plane_sums]
    return pl.pallas_call(
        kernel,
        out_shape=tuple(outs),
        in_specs=[any_] * (ng + nz) + [vm] * (ns + nq),
        out_specs=tuple([any_] * (ng + nz) + [vm] * (ns + nq)),
        scratch_shapes=scratch,
        compiler_params=pltpu.CompilerParams(
            collective_id=number, has_side_effects=True, vmem_limit_bytes=VMEM_LIMIT),
        name=name,
    )(*gathers, *rings, *ring_sums, *plane_sums)


def norm_backward_rule(gradient_of_normalized, centered_input, inverse_root, gain_widened):
    weighted_rows = gain_widened * gradient_of_normalized
    return inverse_root * (
        weighted_rows
        - centered_input * jnp.mean(weighted_rows * centered_input, axis=1, keepdims=True)
    )


SWAP = [(t, t ^ 1) for t in range(8)]


def matmul(a, b, dims, out=F32):
    return lax.dot_general(a, b, (dims, ((), ())), preferred_element_type=F32).astype(out)


def per_device(tokens, gain_mix, in_weight, conv_kernel, out_weight, gain_ffn, gate_weight, up_weight, down_weight, lengths, cotangent):
    dp, t = lax.axis_index("dp"), lax.axis_index("tensor")
    z, yl, c = t // 2, t % 2, dp % 2
    position = t * ROWS + jnp.arange(ROWS)
    live = (position < lengths[0]).astype(F32)[:, None]

    conv_pack = jnp.concatenate([in_weight.reshape(96, 3 * CH), out_weight.T], axis=1)
    wide = lambda w: jnp.pad(w, ((0, 0), (0, FP - FB)))
    gate_pack, up_pack, down_pack = wide(gate_weight), wide(up_weight), wide(down_weight.T)
    small = jnp.zeros((16, 256), BF)
    off = (96 * dp) % 128
    small = lax.dynamic_update_slice(small, jnp.stack([gain_mix, gain_ffn]), (0, off))
    small = lax.dynamic_update_slice(small, conv_kernel, (2, 0))
    small = jnp.concatenate([small] * 6, axis=0)
    grad_out = (live * cotangent.astype(F32)).astype(BF)

    wc, wg, ws, tok_all, gout_all = exchange(
        "first", 0, gathers=(conv_pack, gate_pack, small), rings=(tokens, grad_out)
    )
    pieces = ws[:, :, :, :16].reshape(16, 16, 256)
    at = [(96 * s) % 128 for s in range(16)]
    gains = jnp.concatenate([pieces[s, :2, at[s] : at[s] + 96] for s in range(16)], axis=1).astype(F32)
    g_mix, g_ffn = gains[0], gains[1]
    taps = pieces[0, 2:5, :CH].astype(F32)

    tok_f = tok_all.reshape(1024, D).astype(F32)
    inv1_all = lax.rsqrt(jnp.mean(tok_f * tok_f, axis=1, keepdims=True) + epsilon)
    normed_all = (tok_f * inv1_all * g_mix).astype(BF)
    wc = wc.reshape(D, 768)
    w_in, w_out_t = wc[:, : 3 * CH], wc[:, 3 * CH :]
    projected = matmul(normed_all, w_in, ((1,), (0,)))
    b_gate, c_gate, value = projected[:, :CH], projected[:, CH : 2 * CH], projected[:, 2 * CH :]
    bx = b_gate * value
    bx4 = bx.reshape(2, 4, ROWS, CH)
    halo = lax.ppermute(bx4[:, :, ROWS - 2 :], "tensor", SWAP)
    shifted = jnp.pad(halo, ((0, 0), (1, 0), (0, 0), (0, 0)))[:, :4]
    halo = jnp.where(yl == 1, halo, shifted)
    ext = jnp.concatenate([halo, bx4], axis=2)
    bx_one = ext[:, :, 1:-1].reshape(1024, CH)
    bx_two = ext[:, :, :-2].reshape(1024, CH)
    conv_sum = taps[0] * bx + taps[1] * bx_one + taps[2] * bx_two
    mixed = (c_gate * conv_sum).astype(BF)
    mixer_part = matmul(mixed, w_out_t, ((1,), (1,)), BF)

    wu, mixer_rows = exchange(
        "second", 1, gathers=(up_pack,), ring_sums=(mixer_part.reshape(2, 4, ROWS, D),)
    )
    tok = tokens.astype(F32)
    resid = tok + mixer_rows
    inv2 = lax.rsqrt(jnp.mean(resid * resid, axis=1, keepdims=True) + epsilon)
    xhat2 = resid * inv2
    normed2 = (xhat2 * g_ffn).astype(BF)
    wd, normed2_all = exchange("third", 2, gathers=(down_pack,), rings=(normed2,))
    normed2_all = normed2_all.reshape(1024, D)
    w_gate, w_up, w_down_t = wg.reshape(D, FP), wu.reshape(D, FP), wd.reshape(D, FP)
    gout_all = gout_all.reshape(1024, D)

    gate_pre = matmul(normed2_all, w_gate, ((1,), (0,)))
    up_pre = matmul(normed2_all, w_up, ((1,), (0,)))
    sig = jax.nn.sigmoid(gate_pre)
    silu = gate_pre * sig
    hidden = (silu * up_pre).astype(BF)
    ffn_part = matmul(hidden, w_down_t, ((1,), (1,)), BF)
    grad_act = matmul(gout_all, w_down_t, ((1,), (0,)))
    grad_gate = (grad_act * up_pre * sig * (1.0 + gate_pre * (1.0 - sig))).astype(BF)
    grad_up = (grad_act * silu).astype(BF)
    gn2 = matmul(grad_gate, w_gate, ((1,), (1,))) + matmul(grad_up, w_up, ((1,), (1,)))
    gn2 = gn2.astype(BF)
    gate_full = matmul(normed2_all, grad_gate, ((0,), (0,)), BF)
    up_full = matmul(normed2_all, grad_up, ((0,), (0,)), BF)
    down_full = matmul(gout_all, hidden, ((0,), (0,)), BF)

    as_slots = lambda v: v.reshape(4, 2, 2, 96, v.shape[-1])
    gn2_rows, gate_sum = exchange(
        "fourth", 3, ring_sums=(gn2.reshape(2, 4, ROWS, D),), plane_sums=(as_slots(gate_full),)
    )
    grad_resid = grad_out.astype(F32) + norm_backward_rule(gn2_rows, xhat2, inv2, g_ffn)
    branch_all, up_sum = exchange(
        "fifth", 4, rings=(grad_resid.astype(BF),), plane_sums=(as_slots(up_full),)
    )
    branch_all = branch_all.reshape(1024, D)
    out_full = matmul(branch_all, mixed, ((0,), (0,)), BF)
    grad_mixed = matmul(branch_all, w_out_t, ((1,), (0,)))
    grad_c = grad_mixed * conv_sum
    grad_conv = grad_mixed * c_gate
    gc4 = grad_conv.reshape(2, 4, ROWS, CH)
    ahead = lax.ppermute(gc4[:, :, :2], "tensor", SWAP)
    shifted = jnp.pad(ahead, ((0, 0), (0, 1), (0, 0), (0, 0)))[:, 1:]
    ahead = jnp.where(yl == 0, ahead, shifted)
    ext = jnp.concatenate([gc4, ahead], axis=2)
    grad_bx = (
        taps[0] * grad_conv
        + taps[1] * ext[:, :, 1:-1].reshape(1024, CH)
        + taps[2] * ext[:, :, 2:].reshape(1024, CH)
    )
    kernel_part = jnp.stack(
        [jnp.sum(grad_conv * bx, 0), jnp.sum(grad_conv * bx_one, 0), jnp.sum(grad_conv * bx_two, 0)]
    )
    grad_projected = jnp.concatenate([grad_bx * value, grad_c, grad_bx * b_gate], axis=1).astype(BF)
    in_full = matmul(normed_all, grad_projected, ((0,), (0,)), BF)
    gn1 = matmul(grad_projected, w_in, ((1,), (1,)), BF)
    conv_full = jnp.concatenate([in_full, out_full], axis=1)
    taps_at = jnp.pad(kernel_part.T.reshape(16, 12, 3), ((0, 0), (0, 84), (0, 0))).astype(BF)
    down_full = lax.dynamic_update_slice(down_full, taps_at.reshape(D, 3), (0, FB))
    gn1_rows, ffn_rows, down_sum, conv_sums = exchange(
        "sixth",
        5,
        ring_sums=(gn1.reshape(2, 4, ROWS, D), ffn_part.reshape(2, 4, ROWS, D)),
        plane_sums=(as_slots(down_full), as_slots(conv_full)),
    )
    layer_out = (live * (resid + ffn_rows)).astype(BF)
    inv1 = lax.rsqrt(jnp.mean(tok * tok, axis=1, keepdims=True) + epsilon)
    tokens_grad = (grad_resid + norm_backward_rule(gn1_rows, tok * inv1, inv1, g_mix)).astype(BF)

    in_grad = conv_sums[:, : 3 * CH].reshape(96, 3, CH)
    out_grad = conv_sums[:, 3 * CH :].T
    gate_grad, up_grad = gate_sum[:, :FB], up_sum[:, :FB]
    down_grad = down_sum[:, :FB].T
    mix_share = jnp.sum(in_grad * in_weight.astype(F32), axis=(1, 2)) / gain_mix.astype(F32)
    ffn_share = jnp.sum(
        gate_grad * gate_weight.astype(F32) + up_grad * up_weight.astype(F32), axis=1
    ) / gain_ffn.astype(F32)
    shares = lax.psum_scatter(
        jnp.stack([mix_share, ffn_share]).reshape(2, 8, 12), "tensor", scatter_dimension=1
    )
    move = [(i, (i % 8) * 16 + i // 8) for i in range(128)]
    kernel_grad = lax.ppermute(down_sum[:12, FB : FB + 3].T, ("dp", "tensor"), move)
    return (
        layer_out,
        tokens_grad,
        shares[0],
        in_grad,
        kernel_grad,
        out_grad,
        shares[1],
        gate_grad,
        up_grad,
        down_grad,
    )


def solution(mesh):
    placed = (
        P(("dp", "tensor"), None),
        P("dp"),
        P("dp", None, "tensor"),
        P(None, "tensor"),
        P("tensor", "dp"),
        P("dp"),
        P("dp", "tensor"),
        P("dp", "tensor"),
        P("tensor", "dp"),
        P("dp"),
        P(("dp", "tensor"), None),
    )
    return jax.shard_map(
        per_device,
        mesh=mesh,
        in_specs=placed,
        out_specs=(
            P(("dp", "tensor"), None),
            P(("dp", "tensor"), None),
            P(("dp", "tensor")),
            P("dp", None, "tensor"),
            P(None, ("dp", "tensor")),
            P("tensor", "dp"),
            P(("dp", "tensor")),
            P("dp", "tensor"),
            P("dp", "tensor"),
            P("tensor", "dp"),
        ),
        check_vma=False,
    )
```

time: 1290 us -> 450 us (0.35)
  waiting for transfers between devices: 1000 us -> 4.78 us
  Pallas kernels: 0 us -> 242 us
  blocking collectives: 126 us -> 18.1 us
  local copies, waits for them, and re-layouts: 22.5 us -> 62.8 us
  matrix products: 89.6 us -> 63.3 us
  other arithmetic: 24.8 us -> 41.5 us
  between operations: 15.9 us -> 2.15 us
    reduce_scatter x8 -> x0, waiting for transfers between devices: 550 us -> none  [the longest x1 130 us: per_device(): lax.psum_scatter(mixer_part, 'tensor', scatter_dimension=0, tiled=True)]
    all_gather x8 -> x0, waiting for transfers between devices: 381 us -> none  [the longest x1 73.3 us: per_device(): lax.all_gather(output_gradient.astype(jnp.bfloat16), 'tensor', axis=0, ti...]
    pallas_call x0 -> x6, Pallas kernels: none -> 242 us  [exchange(): pl.pallas_call(kernel, out_shape=tuple(outs), in_specs=[any_] * (ng + nz)...]
    unnamed x2 -> x1, blocking collectives: 97 us -> 18.1 us
    unnamed x18 -> x0, waiting for transfers between devices: 68.4 us -> none
    all_gather x1 -> x0, blocking collectives: 28.9 us -> none  [per_device(): lax.all_gather(out_weight, 'dp', axis=1, tiled=True)]
    dot_general x14 -> x15, matrix products: 85.1 us -> 63.3 us  [matmul(): lax.dot_general(a, b, (dims, ((), ())), preferred_element_type=F32)]
    reshape x0 -> x8, local copies, waits for them, and re-layouts: none -> 13.9 us  [the longest x1 2.62 us: per_device(): bx_one = ext[:, :, 1:-1].reshape(1024, CH)]
  transfers between devices with their start and end apart: 17 -> 3, of which waited for: 16 -> 1; matrix products, arithmetic and copies ran while one was open for 7% -> 5% of each run, Pallas kernels for 0% -> 0%
where the time goes in v1:
time: 450 us; the launch traced here: 441 us
  Pallas kernels  242 us (54%)
  matrix products  63.3 us (14%)
  local copies, waits for them, and re-layouts  62.8 us (14%)
  other arithmetic  41.5 us (9%)
  blocking collectives  18.1 us (4%)
  starting transfers between devices  6.63 us (1%)
  waiting for transfers between devices  4.78 us (1%)
    pallas_call x6, Pallas kernels, exchange(): pl.pallas_call(kernel, out_shape=tuple(outs), in_specs=[any_] * (ng + nz)...  242 us
    dot_general x15, matrix products, matmul(): lax.dot_general(a, b, (dims, ((), ())), preferred_element_type=F32)  63.3 us
    unnamed x1, blocking collectives  18.1 us
    unnamed x89, local copies, waits for them, and re-layouts  15.3 us
  transfers between devices with their start and end apart: 3, of which 1 were waited for; matrix products, arithmetic and copies ran while one was open for 5% of the time, Pallas kernels for 0%

profile of v1, /device:TPU:30, one launch (start us, length us, event | category | flops | bytes accessed | tf_op | source)
XLA Modules:
  0.0 441.1 jit_solution(11096624943382037488)
XLA Ops:
  8.8 1.9 multiply_convert_fusion.9.refs_4_
  10.7 61.7 %first.1 = (bf16[4,2,2,96,768]{4,3,2,1,0:T(8,128)(2,1)}, bf16[4,2,2,96,896]{4,3,2,1,0:T(8,128)(2,1)}, bf16[4,2,2,96,256]{4,3,2,1,0:T(8,128)(2,1)}, bf16[2,4,128,...) custom-call(bf16[96,768]{1,0:T(8,128)(2,1)} %pad_maximum_fusion.6.refs_0_, bf16[96,896]{1,0:T(8,128)(2,1)} %pad.24.refs_1_, ...), custom_call_target="tpu_custom_call" | custom-call | tf_op jit(solution)/shard_map/first/pallas_call | solution.py:413
  74.4 2.6 multiply_reduce_fusion
  78.6 2.1 fusion.4
  82.1 2.5 slice.208
  86.1 2.1 collective-permute-start
  92.9 4.3 fusion.15
  98.7 2.6 reshape.169
  101.3 2.3 multiply_convert_fusion.8
  104.4 4.3 convolution_convert_fusion.1
  108.6 35.7 %second.1 = (bf16[4,2,2,96,896]{4,3,2,1,0:T(8,128)(2,1)}, f32[128,1536]{1,0:T(8,128)}) custom-call(bf16[96,896]{1,0:T(8,128)(2,1)} %pad.23.refs_0_, bf16[2,4,128,1536]{3,2,1,0:T(8,128)(2,1)} %bitcast.121), custom_call_target="tpu_custom_call" | custom-call | tf_op jit(solution)/shard_map/second/pallas_call | solution.py:413
  145.6 2.0 multiply_convert_fusion.7.refs_1_
  147.6 38.1 %third.1 = (bf16[4,2,2,96,896]{4,3,2,1,0:T(8,128)(2,1)}, bf16[2,4,128,1536]{3,2,1,0:T(8,128)(2,1)}) custom-call(bf16[96,896]{1,0:T(8,128)(2,1)} %pad.26.refs_0_, bf16[128,1536]{1,0:T(8,128)(2,1)} %multiply_convert_fusion.7.refs_1_), custom_call_target="tpu_custom_call" | custom-call | tf_op jit(solution)/shard_map/third/pallas_call | solution.py:413
  185.8 6.3 %fusion.26 = f32[1024,896]{1,0:T(8,128)S(1)} fusion(bf16[1024,1536]{1,0:T(8,128)(2,1)} %bitcast.151, bf16[1536,896]{1,0:T(8,128)(2,1)} %bitcast.155), kind=kOutput, calls=%fused_computation.116 | convolution fusion | flops 2818572288 | bytes 9568256 | tf_op jit(solution)/shard_map/dot_general | solution.py:437
  192.1 3.4 fusion.25
  195.5 4.9 %multiply_convert_fusion = (bf16[1024,896]{1,0:T(8,128)(2,1)S(1)}, bf16[1024,896]{1,0:T(8,128)(2,1)S(1)}, bf16[1024,896]{1,0:T(8,128)(2,1)S(1)}) fusion(f32[1024,896]{1,0:T(8,128)S(1)} %fusion.26, f32[1024,896]{1,0:T(8,128)S(1)} %fusion.25, bf16[1024,1536]{1,0:T(8,128)(2,1)S(1)} %bitcast.152, bf16[1536,896]{1,0:T(8,128)(2,1)S(1)} %bitcast.157), kind=kOutput, calls=%fused_computation.8 | convolution fusion | flops 2832334848 | bytes 18743296 | tf_op jit(solution)/shard_map/dot_general | solution.py:437
  200.4 3.4 fusion.27
  203.9 4.8 %convolution_convert_fusion.5 = bf16[1536,896]{1,0:T(8,128)(2,1)} fusion(bf16[1024,1536]{1,0:T(8,128)(2,1)S(1)} %bitcast.153, bf16[1024,896]{1,0:T(8,128)(2,1)S(1)} %get-tuple-element.90), kind=kOutput, calls=%fused_computation.15 | convolution fusion | flops 2819948544 | bytes 7733248 | tf_op jit(solution)/shard_map/dot_general | solution.py:437
  208.7 4.9 %convolution_convert_fusion.2 = bf16[1024,1536]{1,0:T(8,128)(2,1)} fusion(bf16[1024,896]{1,0:T(8,128)(2,1)S(1)} %get-tuple-element.89, bf16[1536,896]{1,0:T(8,128)(2,1)S(1)} %bitcast.160), kind=kOutput, calls=%fused_computation.7 | convolution fusion | flops 2820145152 | bytes 7733248 | tf_op jit(solution)/shard_map/dot_general | solution.py:437
  213.6 4.8 %convolution_convert_fusion.3 = bf16[1536,896]{1,0:T(8,128)(2,1)} fusion(bf16[1024,1536]{1,0:T(8,128)(2,1)S(1)} %bitcast.150, bf16[1024,896]{1,0:T(8,128)(2,1)S(1)} %get-tuple-element.89), kind=kOutput, calls=%fused_computation.13 | convolution fusion | flops 2819948544 | bytes 7733248 | tf_op jit(solution)/shard_map/dot_general | solution.py:437
  218.4 4.8 %convolution_convert_fusion.4 = bf16[1536,896]{1,0:T(8,128)(2,1)} fusion(bf16[1024,1536]{1,0:T(8,128)(2,1)S(1)} %bitcast.154, bf16[1024,896]{1,0:T(8,128)(2,1)S(1)} %get-tuple-element.91), kind=kOutput, calls=%fused_computation.14 | convolution fusion | flops 2819948544 | bytes 7733248 | tf_op jit(solution)/shard_map/dot_general | solution.py:437
  223.3 4.9 %add_convert_fusion = bf16[1024,1536]{1,0:T(8,128)(2,1)} fusion(f32[1024,1536]{1,0:T(8,128)S(1)} %fusion.27, bf16[1024,896]{1,0:T(8,128)(2,1)S(1)} %get-tuple-element.91, bf16[1536,896]{1,0:T(8,128)(2,1)S(1)} %bitcast.158), kind=kOutput, calls=%fused_computation.3 | convolution fusion | flops 2821718016 | bytes 14024704 | tf_op jit(solution)/shard_map/dot_general | solution.py:437
  228.2 31.4 %fourth.1 = (f32[128,1536]{1,0:T(8,128)}, f32[96,896]{1,0:T(8,128)}) custom-call(bf16[2,4,128,1536]{3,2,1,0:T(8,128)(2,1)} %bitcast.124, bf16[4,2,2,96,896]{4,3,2,1,0:T(8,128)(2,1)} %bitcast.129), custom_call_target="tpu_custom_call" | custom-call | tf_op jit(solution)/shard_map/fourth/pallas_call | solution.py:413
  261.6 2.2 fusion.23.refs_0_
  263.8 32.5 %fifth.1 = (bf16[2,4,128,1536]{3,2,1,0:T(8,128)(2,1)}, f32[96,896]{1,0:T(8,128)}) custom-call(bf16[128,1536]{1,0:T(8,128)(2,1)} %fusion.23.refs_0_, bf16[4,2,2,96,896]{4,3,2,1,0:T(8,128)(2,1)} %bitcast.128), custom_call_target="tpu_custom_call" | custom-call | tf_op jit(solution)/shard_map/fifth/pallas_call | solution.py:413
  296.3 3.7 convolution_convert_fusion.7
  300.0 4.8 %multiply_reduce_fusion.3 = (bf16[192]{0:T(256)(128)(2,1)}, bf16[192]{0:T(256)(128)(2,1)}, bf16[192]{0:T(256)(128)(2,1)}, f32[1024,192]{0,1:T(8,128)}, bf16[1024,192]{0,1:T(8,128)(2,1)}) fusion(f32[1024,192]{0,1:T(8,128)S(1)} %copy-done.5, f32[1024,192]{0,1:T(8,128)} %copy-done.7, f32[1024,192]{0,1:T(8,128)} %reshape.169, f32[1024,576]{0,1:T(8,128)S(1)} %fusion.4, ...), kind=kOutput, calls=%fused_computation.45 | convolution fusion | flops 605748672 | bytes 9045120 | tf_op jit(solution)/shard_map/dot_general | solution.py:437
  304.9 2.4 reshape.181
  307.2 2.1 copy.54
  309.3 2.6 collective-permute-start.1
  313.9 2.3 add_reduce_fusion
  320.9 1.6 pad.28.clone
  323.8 4.7 %dynamic_update_slice.11 = bf16[1536,896]{1,0:T(8,128)(2,1)} dynamic-update-slice(bf16[1536,896]{1,0:T(8,128)(2,1)} %convolution_convert_fusion.3, bf16[1536,3]{1,0:T(8,128)(2,1)} %bitcast.132, s32[]{:T(128)} %constant.47.clone.1, s32[]{:T(128)} %constant.59.clone.1) | dynamic-update-slice | bytes 18436 | tf_op jit(solution)/shard_map/dynamic_update_slice | solution.py:543
  330.0 1.9 copy.44
  331.9 4.7 %fusion.14 = (f32[2,4,128,192]{2,1,0,3:T(4,128)}, f32[2,4,128,192]{2,1,0,3:T(4,128)}) fusion(f32[2,4,128,192]{2,1,0,3:T(4,128)} %reshape.181, f32[2,4,2,192]{2,1,0,3:T(4,128)} %copy.44), kind=kLoop, calls=%fused_computation.38 | loop fusion | flops 393216 | bytes 2371584 | tf_op jit(solution)/shard_map/concatenate | solution.py:529
  336.6 2.3 reshape.183
  339.0 2.4 reshape.182
  341.3 2.0 multiply_convert_fusion.6
  343.8 4.2 convolution_convert_fusion
  347.9 2.0 convolution_convert_fusion.6
  350.1 2.4 copy.46
  352.5 42.4 %sixth.1 = (f32[128,1536]{1,0:T(8,128)}, f32[128,1536]{1,0:T(8,128)}, f32[96,896]{1,0:T(8,128)}, f32[96,768]{1,0:T(8,128)}) custom-call(bf16[2,4,128,1536]{3,2,1,0:T(8,128)(2,1)} %bitcast.126, bf16[2,4,128,1536]{3,2,1,0:T(8,128)(2,1)} %bitcast.125, bf16[4,2,2,96,896]{4,3,2,1,0:T(8,128)(2,1)} %bitcast.127, bf16[4,2,2,96,768]{4,3,2,1,0:T(8,128)(2,1)} %bitcast.122), custom_call_target="tpu_custom_call" | custom-call | tf_op jit(solution)/shard_map/sixth/pallas_call | solution.py:413
  394.9 1.8 slice.176
  399.1 1.7 slice_bitcast_fusion
  408.6 18.1 %all-reduce.6 = f32[2,8,12]{2,0,1:T(2,128)} all-reduce(f32[2,8,12]{2,0,1:T(2,128)} %copy.49), channel_id=2, replica_groups=mesh['dp'=16,'tensor'=8] {'tensor'}, use_global_device_ids=true, to_apply=%region_10.11.clone | all-reduce | flops 192 | bytes 1536
  428.5 1.9 collective-permute-start.2
  430.5 2.7 fusion.12
  434.8 4.8 %collective-permute-done.2 = f32[3,12]{0,1:T(8,128)} collective-permute-done((f32[3,12]{0,1:T(8,128)}, f32[3,12]{0,1:T(8,128)}, u32[]{:S(2)}, u32[]{:S(2)}) %collective-permute-start.2) | collective-permute-done | bytes 176 | tf_op jit(solution)/shard_map/ppermute | solution.py:566
  (140 shorter events, 48.9 us)
Async XLA Ops:
  2.6 8.0 %copy-start.16 = (bf16[96,3,192]{0,2,1:T(8,128)(2,1)}, bf16[96,3,192]{0,2,1:T(8,128)(2,1)S(1)}, u32[]{:S(2)}) copy-start(bf16[96,3,192]{0,2,1:T(8,128)(2,1)S(1)} %copy.38) | copy-start | bytes 331780
  7.3 3.3 copy-start.23
  8.8 1.9 copy-start.30
  72.4 4.6 %copy-start.3 = (bf16[2,4,128,1536]{3,2,1,0:T(8,128)(2,1)S(1)}, bf16[2,4,128,1536]{3,2,1,0:T(8,128)(2,1)}, u32[]{:S(2)}) copy-start(bf16[2,4,128,1536]{3,2,1,0:T(8,128)(2,1)} %get-tuple-element.27) | copy-start | bytes 9437188
  73.5 0.7 copy-start.22
  77.0 1.7 copy-start.17
  77.8 3.0 copy-start.13
  80.7 8.2 %copy-start.19 = (bf16[96,864]{1,0:T(8,128)(2,1)S(1)}, bf16[96,864]{1,0:T(8,128)(2,1)}, u32[]{:S(2)}) copy-start(bf16[96,864]{1,0:T(8,128)(2,1)} %param.18) | copy-start | bytes 497668
  80.9 12.0 %copy-start.4 = (f32[1024,192]{0,1:T(8,128)}, f32[1024,192]{0,1:T(8,128)S(1)}, u32[]{:S(2)}) copy-start(f32[1024,192]{0,1:T(8,128)S(1)} %slice_multiply_fusion) | copy-start | bytes 2359300
  80.9 8.8 %copy-start.21 = (bf16[864,96]{0,1:T(8,128)(2,1)S(1)}, bf16[864,96]{0,1:T(8,128)(2,1)}, u32[]{:S(2)}) copy-start(bf16[864,96]{0,1:T(8,128)(2,1)} %param.19) | copy-start | bytes 497668
  86.1 5.5 %collective-permute-start = (f32[2,4,2,192]{3,1,2,0:T(4,128)S(1)}, f32[2,4,2,192]{3,1,2,0:T(4,128)S(1)}, u32[]{:S(2)}, u32[]{:S(2)}) collective-permute-start(f32[2,4,2,192]{3,1,2,0:T(4,128)S(1)} %copy.53), channel_id=1, source_target_pairs={{0,1},{1,0},{2,3},{3,2},{4,5},{5,4},{6,7},{7,6},{8,9},{9,8},{10,11... | collective-permute-start | bytes 36872 | tf_op jit(solution)/shard_map/ppermute | solution.py:474
  88.9 12.4 %copy-start.24 = (f32[1,1,192]{2,1,0:T(1,128)}, f32[1,1,192]{2,1,0:T(1,128)S(1)}, u32[]{:S(2)}) copy-start(f32[1,1,192]{2,1,0:T(1,128)S(1)} %get-tuple-element.115) | copy-start | bytes 2308
  88.9 12.4 %copy-start.25 = (f32[1,1,192]{2,1,0:T(1,128)}, f32[1,1,192]{2,1,0:T(1,128)S(1)}, u32[]{:S(2)}) copy-start(f32[1,1,192]{2,1,0:T(1,128)S(1)} %get-tuple-element.116) | copy-start | bytes 2308
  88.9 12.4 %copy-start.26 = (f32[1,1,192]{2,1,0:T(1,128)}, f32[1,1,192]{2,1,0:T(1,128)S(1)}, u32[]{:S(2)}) copy-start(f32[1,1,192]{2,1,0:T(1,128)S(1)} %get-tuple-element.117) | copy-start | bytes 2308
  98.7 4.9 %copy-start.7 = (f32[1024,192]{0,1:T(8,128)}, f32[1024,192]{0,1:T(8,128)S(1)}, u32[]{:S(2)}) copy-start(f32[1024,192]{0,1:T(8,128)S(1)} %reshape.170) | copy-start | bytes 2359300
  103.6 0.7 copy-start.10
  104.3 39.9 %copy-start.1 = (bf16[128,1536]{1,0:T(8,128)(2,1)S(1)}, bf16[128,1536]{1,0:T(8,128)(2,1)}, u32[]{:S(2)}) copy-start(bf16[128,1536]{1,0:T(8,128)(2,1)} %refs_3_.1) | copy-start | bytes 1179652
  145.6 116.0 %copy-start.27 = (f32[128]{0:T(128)}, f32[128]{0:T(128)S(1)}, u32[]{:S(2)}) copy-start(f32[128]{0:T(128)S(1)} %add_rsqrt_fusion.2) | copy-start | bytes 1540
  185.7 6.3 %copy-start.32 = (bf16[2,4,128,1536]{3,2,1,0:T(8,128)(2,1)S(1)}, bf16[2,4,128,1536]{3,2,1,0:T(8,128)(2,1)}, u32[]{:S(2)}) copy-start(bf16[2,4,128,1536]{3,2,1,0:T(8,128)(2,1)} %get-tuple-element.31) | copy-start | bytes 9437188
  185.7 6.3 %copy-start.36 = (bf16[4,2,2,96,896]{4,3,2,1,0:T(8,128)(2,1)S(1)}, bf16[4,2,2,96,896]{4,3,2,1,0:T(8,128)(2,1)}, u32[]{:S(2)}) copy-start(bf16[4,2,2,96,896]{4,3,2,1,0:T(8,128)(2,1)} %get-tuple-element.32) | copy-start | bytes 8257540
  192.1 3.4 copy-start.33
  192.1 3.4 copy-start.35
  195.5 4.9 %copy-start.34 = (bf16[4,2,2,96,896]{4,3,2,1,0:T(8,128)(2,1)S(1)}, bf16[4,2,2,96,896]{4,3,2,1,0:T(8,128)(2,1)}, u32[]{:S(2)}) copy-start(bf16[4,2,2,96,896]{4,3,2,1,0:T(8,128)(2,1)} %get-tuple-element.35) | copy-start | bytes 8257540
  228.2 31.4 %copy-start = (f32[128,1536]{1,0:T(8,128)S(1)}, f32[128,1536]{1,0:T(8,128)}, u32[]{:S(2)}) copy-start(f32[128,1536]{1,0:T(8,128)} %get-tuple-element.30) | copy-start | bytes 2359300
  228.2 33.4 %copy-start.8 = (bf16[128,1536]{1,0:T(8,128)(2,1)S(1)}, bf16[128,1536]{1,0:T(8,128)(2,1)}, u32[]{:S(2)}) copy-start(bf16[128,1536]{1,0:T(8,128)(2,1)} %param.21) | copy-start | bytes 1179652
  228.2 33.4 %copy-start.31 = (f32[128]{0:T(128)S(1)}, f32[128]{0:T(128)}, u32[]{:S(2)}) copy-start(f32[128]{0:T(128)} %copy-done.30) | copy-start | bytes 1540
  261.6 34.7 %copy-start.29 = (f32[128]{0:T(128)}, f32[128]{0:T(128)S(1)}, u32[]{:S(2)}) copy-start(f32[128]{0:T(128)S(1)} %get-tuple-element.121) | copy-start | bytes 1540
  263.8 32.5 %copy-start.11 = (bf16[1024,192]{0,1:T(8,128)(2,1)S(1)}, bf16[1024,192]{0,1:T(8,128)(2,1)}, u32[]{:S(2)}) copy-start(bf16[1024,192]{0,1:T(8,128)(2,1)} %copy-done.10) | copy-start | bytes 1179652
  296.3 3.7 copy-start.2
  296.3 3.7 copy-start.5
  309.3 19.3 %collective-permute-start.1 = (f32[2,4,2,192]{3,1,2,0:T(4,128)}, f32[2,4,2,192]{3,1,2,0:T(4,128)}, u32[]{:S(2)}, u32[]{:S(2)}) collective-permute-start(f32[2,4,2,192]{3,1,2,0:T(4,128)} %copy.54), channel_id=1, source_target_pairs={{0,1},{1,0},{2,3},{3,2},{4,5},{5,4},{6,7},{7,6},{8,9},{9,8},{10,11... | collective-permute-start | bytes 36872 | tf_op jit(solution)/shard_map/ppermute | solution.py:526
  341.3 2.4 copy-start.18
  341.3 2.4 copy-start.20
  343.8 4.2 copy-start.14
  347.9 2.0 copy-start.15
  352.5 48.3 %copy-start.28 = (f32[128]{0:T(128)S(1)}, f32[128]{0:T(128)}, u32[]{:S(2)}) copy-start(f32[128]{0:T(128)} %get-tuple-element.120) | copy-start | bytes 1540
  394.9 35.6 %copy-start.6 = (f32[128,1536]{1,0:T(8,128)S(1)}, f32[128,1536]{1,0:T(8,128)}, u32[]{:S(2)}) copy-start(f32[128,1536]{1,0:T(8,128)} %get-tuple-element.36) | copy-start | bytes 2359300
  394.9 35.6 %copy-start.9 = (bf16[128,1536]{1,0:T(8,128)(2,1)S(1)}, bf16[128,1536]{1,0:T(8,128)(2,1)}, u32[]{:S(2)}) copy-start(bf16[128,1536]{1,0:T(8,128)(2,1)} %param.21) | copy-start | bytes 1179652
  394.9 35.6 %copy-start.12 = (f32[128,1536]{1,0:T(8,128)S(1)}, f32[128,1536]{1,0:T(8,128)}, u32[]{:S(2)}) copy-start(f32[128,1536]{1,0:T(8,128)} %get-tuple-element.39) | copy-start | bytes 2359300
  428.5 11.0 %collective-permute-start.2 = (f32[3,12]{0,1:T(8,128)}, f32[3,12]{0,1:T(8,128)}, u32[]{:S(2)}, u32[]{:S(2)}) collective-permute-start(f32[3,12]{0,1:T(8,128)} %slice_bitcast_fusion.2), channel_id=1, source_target_pairs={{0,0},{1,16},{2,32},{3,48},{4,64},{5,80},{6,96},{7,112},{8,1},{9,1... | collective-permute-start | bytes 440 | tf_op jit(solution)/shard_map/ppermute | solution.py:566

commit v2 on v1

v2 whole, which is shorter than its diff:
```python
import functools

import jax
import jax.numpy as jnp
from jax import lax
from jax.experimental import pallas as pl
from jax.experimental.pallas import tpu as pltpu
from jax.sharding import PartitionSpec as P

epsilon = 1e-05
MESH = pl.DeviceIdType.MESH
BF = jnp.bfloat16
F32 = jnp.float32
D = 1536
ROWS = 128
CH = 192
FB = 864
FP = 896
HALF = 48
VMEM_LIMIT = 60 << 20


class Place:
    def __init__(self):
        dp = lax.axis_index("dp")
        t = lax.axis_index("tensor")
        self.x, self.yh, self.c = dp // 4, (dp // 2) % 2, dp % 2
        self.z, self.yl = t // 2, t % 2
        self.y = self.yh * 2 + self.yl
        self.o = 1 - self.c
        self.xp, self.xm, self.x2 = (self.x + 1) % 4, (self.x + 3) % 4, (self.x + 2) % 4
        self.yp, self.ym = (self.y + 1) % 4, (self.y + 3) % 4
        self.yhp, self.yhm = self.yp // 2, self.ym // 2
        self.way = 1 - 2 * self.c
        self.zf = (self.z + self.way + 4) % 4
        self.zb = (self.z - self.way + 4) % 4
        self.zp, self.zm, self.z2 = (self.z + 1) % 4, (self.z + 3) % 4, (self.z + 2) % 4
        self.own = self.c == self.yl
        self.opp = self.c != self.yl

    def at(self, x=None, y=None, z=None, c=None):
        x = self.x if x is None else x
        y = self.y if y is None else y
        z = self.z if z is None else z
        c = self.c if c is None else c
        return (x * 4 + (y // 2) * 2 + c, z * 2 + y % 2)


class Net:
    def __init__(self, place, send, recv, local=None):
        self.p, self.ss, self.rs, self.ls = place, send, recv, local
        self.ns = self.nr = self.nl = 0
        self.pending = []

    def sem(self, n=1):
        k = self.nr
        self.nr += n
        return k

    def send(self, src, dst, recv_index, target, cond=None):
        k = self.ns
        self.ns += 1
        d = pltpu.make_async_remote_copy(
            src_ref=src, dst_ref=dst, send_sem=self.ss.at[k], recv_sem=self.rs.at[recv_index],
            device_id=target, device_id_type=MESH)
        run(cond, d.start)
        self.pending.append((cond, d))

    def copy(self, src, dst, cond=None):
        k = self.nl
        self.nl += 1
        d = pltpu.make_async_copy(src, dst, self.ls.at[k])
        run(cond, d.start)
        return lambda: run(cond, d.wait)

    def got(self, dst, recv_index, cond=None):
        d = pltpu.make_async_remote_copy(
            src_ref=dst, dst_ref=dst, send_sem=self.ss.at[0], recv_sem=self.rs.at[recv_index],
            device_id=self.p.at(c=self.p.o), device_id_type=MESH)
        run(cond, d.wait_recv)

    def finish(self):
        for cond, d in self.pending:
            run(cond, d.wait_send)
        self.pending = []


def run(cond, f):
    if cond is None:
        f()
    else:
        pl.when(cond)(f)


def greet(p, plane, ring):
    bar = pltpu.get_barrier_semaphore()
    who = [p.at(c=p.o)]
    if plane:
        for c in (0, 1):
            who += [p.at(x=p.xp, c=c), p.at(x=p.xm, c=c), p.at(y=p.yp, c=c), p.at(y=p.ym, c=c)]
    if ring:
        who += [p.at(z=p.zp), p.at(z=p.zm)]
    for w in who:
        pl.semaphore_signal(bar, inc=1, device_id=w, device_id_type=MESH)
    pl.semaphore_wait(bar, len(who))


def together(*jobs):
    jobs = list(jobs)
    while jobs:
        for j in list(jobs):
            try:
                next(j)
            except StopIteration:
                jobs.remove(j)


HA, HB = pl.ds(0, HALF), pl.ds(HALF, HALF)


def add(out, *terms):
    lead = out.shape[:-2]
    count = 1
    for s in lead:
        count *= s

    def one(i):
        at = []
        for s in reversed(lead):
            at.append(i % s)
            i = i // s
        at = tuple(reversed(at))
        v = terms[0][at].astype(F32) if at else terms[0][...].astype(F32)
        for t in terms[1:]:
            v = v + (t[at] if at else t[...]).astype(F32)
        if at:
            out[at] = v.astype(out.dtype)
        else:
            out[...] = v.astype(out.dtype)

    if not lead:

        def rows(i, _):
            at = pl.ds(pl.multiple_of(i * 16, 16), 16)
            v = terms[0][at].astype(F32)
            for t in terms[1:]:
                v = v + t[at].astype(F32)
            out[at] = v.astype(out.dtype)

        lax.fori_loop(0, out.shape[0] // 16, rows, None)
    else:
        lax.fori_loop(0, count, lambda i, _: one(i), None)


def plane_scratch(n):
    return [
        pltpu.VMEM((2, 4, HALF, n), BF),
        pltpu.VMEM((2, 4, 2, HALF, n), BF),
        pltpu.VMEM((2, HALF, n), BF),
        pltpu.VMEM((3, HALF, n), BF),
        pltpu.VMEM((2, 2, HALF, n), BF),
        pltpu.VMEM((2, 2, 2, HALF, n), BF),
        pltpu.VMEM((2, HALF, n), BF),
        pltpu.VMEM((3, HALF, n), BF),
    ]


def reduce_plane(net, G, out, RA, RB, RC, F, RX, RY, RZ, H):
    p = net.p
    a0, a1, bp0, bp1, bm0, bm1, c0, c1, g0, g1, g2 = (net.sem() for _ in range(11))
    u0, u1, vp0, vp1, vm0, vm1, w0, w1, h0, h1, h2 = (net.sem() for _ in range(11))
    net.send(G.at[:, 1 - p.yh, 0, HA], RA.at[0], a0, p.at(y=p.ym), p.own)
    net.send(G.at[:, 1 - p.yh, 1, HA], RA.at[1], a1, p.at(y=p.yp), p.own)
    net.send(G.at[p.x2, :, 0, HB], RX.at[0], u0, p.at(x=p.xm))
    net.send(G.at[p.x2, :, 1, HB], RX.at[1], u1, p.at(x=p.xp))
    net.send(G.at[:, p.yhm, 1, HA], RB.at[0, :, 1], bp1, p.at(y=p.ym), p.opp)
    net.send(G.at[:, p.yhp, 0, HA], RB.at[1, :, 0], bm0, p.at(y=p.yp), p.opp)
    net.send(G.at[p.xm, :, 1, HB], RY.at[0, :, 1], vp1, p.at(x=p.xm))
    net.send(G.at[p.xp, :, 0, HB], RY.at[1, :, 0], vm0, p.at(x=p.xp))
    yield

    net.got(RA.at[0], a0, p.opp)
    net.got(RA.at[1], a1, p.opp)

    @pl.when(p.opp)
    def _():
        add(RA.at[0], RA.at[0], G.at[:, p.yhm, 0, HA])
        add(RA.at[1], RA.at[1], G.at[:, p.yhp, 1, HA])

    net.send(RA.at[0], RB.at[0, :, 0], bp0, p.at(y=p.ym), p.opp)
    net.send(RA.at[1], RB.at[1, :, 1], bm1, p.at(y=p.yp), p.opp)
    net.got(RX.at[0], u0)
    add(RX.at[0], RX.at[0], G.at[p.xm, :, 0, HB])
    net.send(RX.at[0], RY.at[0, :, 0], vp0, p.at(x=p.xm))
    net.got(RX.at[1], u1)
    add(RX.at[1], RX.at[1], G.at[p.xp, :, 1, HB])
    net.send(RX.at[1], RY.at[1, :, 1], vm1, p.at(x=p.xp))
    yield

    net.got(RB.at[0, :, 1], bp1, p.own)
    net.got(RB.at[1, :, 0], bm0, p.own)
    net.got(RB.at[0, :, 0], bp0, p.own)
    net.got(RB.at[1, :, 1], bm1, p.own)

    @pl.when(p.own)
    def _():
        add(RB.at[0], RB.at[0], RB.at[1], G.at[:, p.yh, :, HA])

    S = RB.at[0]
    net.send(S.at[p.x2, 0], RC.at[0], c0, p.at(x=p.xm), p.own)
    net.send(S.at[p.x2, 1], RC.at[1], c1, p.at(x=p.xp), p.own)
    net.send(S.at[p.xm, 1], F.at[1], g1, p.at(x=p.xm, c=1), p.own)
    net.send(S.at[p.xp, 0], F.at[2], g2, p.at(x=p.xp, c=0), p.own)
    net.send(S.at[p.x, p.o], F.at[0], g0, p.at(c=p.o), p.own)

    net.got(RY.at[0, :, 1], vp1)
    net.got(RY.at[1, :, 0], vm0)
    net.got(RY.at[0, :, 0], vp0)
    net.got(RY.at[1, :, 1], vm1)
    add(RY.at[0], RY.at[0], RY.at[1], G.at[p.x, :, :, HB])
    T = RY.at[0]
    net.send(T.at[1 - p.yh, 0], RZ.at[0], w0, p.at(y=p.ym), p.own)
    net.send(T.at[1 - p.yh, 1], RZ.at[1], w1, p.at(y=p.yp), p.own)
    net.send(T.at[p.yhm, 1], H.at[1], h1, p.at(y=p.ym, c=1), p.opp)
    net.send(T.at[p.yhp, 0], H.at[2], h2, p.at(y=p.yp, c=0), p.opp)
    net.send(T.at[p.yh, p.o], H.at[0], h0, p.at(c=p.o), p.own)
    yield

    net.got(RC.at[0], c0, p.own)
    net.got(RC.at[1], c1, p.own)
    net.got(RZ.at[0], w0, p.opp)
    net.got(RZ.at[1], w1, p.opp)

    @pl.when(p.own)
    def _():
        add(RC.at[0], RC.at[0], S.at[p.xm, 0])
        add(RC.at[1], RC.at[1], S.at[p.xp, 1])

    @pl.when(p.opp)
    def _():
        add(RZ.at[0], RZ.at[0], T.at[p.yhm, 0])
        add(RZ.at[1], RZ.at[1], T.at[p.yhp, 1])

    net.send(RC.at[0], F.at[1], g1, p.at(x=p.xm, c=0), p.own)
    net.send(RC.at[1], F.at[2], g2, p.at(x=p.xp, c=1), p.own)
    net.send(RZ.at[0], H.at[1], h1, p.at(y=p.ym, c=0), p.opp)
    net.send(RZ.at[1], H.at[2], h2, p.at(y=p.yp, c=1), p.opp)
    yield

    net.got(F.at[0], g0, p.opp)
    net.got(F.at[1], g1)
    net.got(F.at[2], g2)
    net.got(H.at[0], h0, p.opp)
    net.got(H.at[1], h1)
    net.got(H.at[2], h2)

    @pl.when(p.own)
    def _():
        F[0] = S[p.x, p.c]
        H[0] = T[p.yh, p.c]

    add(out.at[HA], F.at[0], F.at[1], F.at[2])
    add(out.at[HB], H.at[0], H.at[1], H.at[2])


def ring_scratch(n):
    return [pltpu.VMEM((4, ROWS, n), BF), pltpu.VMEM((2, ROWS, n), BF), pltpu.VMEM((3, ROWS, n), BF)]


def shape(s, t=BF):
    return jax.ShapeDtypeStruct(s, t)


def slots(n):
    return shape((4, 2, 2, 96, n))


def blocks(n):
    return shape((4, 2, ROWS, n))


def gather_plane(net, sh, W):
    p = net.p
    h = sh.shape[0] // 2
    HA, HB = pl.ds(0, h), pl.ds(h, h)
    i_own, f1, f2, f3, f4 = net.sem(), net.sem(2), net.sem(2), net.sem(2), net.sem(2)
    r1, r2, r3, r4, y1, y2, y3, y4, x1, x2, x3, x4 = (net.sem() for _ in range(12))
    q = p.yl
    done = net.copy(sh, W.at[p.x, p.yh, p.c], p.own)
    net.send(sh.at[HA], W.at[p.x, p.yh, p.c, HA], f1 + p.c, p.at(x=p.xp, c=q))
    net.send(sh.at[HA], W.at[p.x, p.yh, p.c, HA], f2 + p.c, p.at(x=p.xm, c=q))
    net.send(sh.at[HB], W.at[p.x, p.yh, p.c, HB], f3 + p.c, p.at(y=p.yp, c=q))
    net.send(sh.at[HB], W.at[p.x, p.yh, p.c, HB], f4 + p.c, p.at(y=p.ym, c=q))
    net.send(sh, W.at[p.x, p.yh, p.c], i_own, p.at(c=p.o), p.opp)
    yield
    net.got(W.at[p.xm, p.yh, 0, HA], f1 + 0, p.own)
    net.got(W.at[p.x, p.yhm, 0, HB], f3 + 0, p.opp)
    net.send(W.at[p.xm, p.yh, 0, HA], W.at[p.xm, p.yh, 0, HA], r1, p.at(x=p.xp), p.own)
    net.send(W.at[p.x, p.yhm, 0, HB], W.at[p.x, p.yhm, 0, HB], r3, p.at(y=p.yp), p.opp)
    net.got(W.at[p.xp, p.yh, 1, HA], f2 + 1, p.own)
    net.got(W.at[p.x, p.yhp, 1, HB], f4 + 1, p.opp)
    net.send(W.at[p.xp, p.yh, 1, HA], W.at[p.xp, p.yh, 1, HA], r2, p.at(x=p.xm), p.own)
    net.send(W.at[p.x, p.yhp, 1, HB], W.at[p.x, p.yhp, 1, HB], r4, p.at(y=p.ym), p.opp)
    yield
    done()
    net.got(W.at[p.x, p.yh, p.o], i_own, p.own)
    net.got(W.at[p.xm, p.yh, 1, HA], f1 + 1, p.own)
    net.got(W.at[p.xp, p.yh, 0, HA], f2 + 0, p.own)
    net.got(W.at[p.x, p.yhm, 1, HB], f3 + 1, p.opp)
    net.got(W.at[p.x, p.yhp, 0, HB], f4 + 0, p.opp)
    net.got(W.at[p.x2, p.yh, 0, HA], r1, p.own)
    net.got(W.at[p.x2, p.yh, 1, HA], r2, p.own)
    net.send(W.at[:, p.yh, :, HA], W.at[:, p.yh, :, HA], y1, p.at(y=p.yp), p.own)
    net.send(W.at[:, p.yh, :, HA], W.at[:, p.yh, :, HA], y2, p.at(y=p.ym), p.own)
    net.got(W.at[p.x, 1 - p.yh, 0, HB], r3, p.own)
    net.got(W.at[p.x, 1 - p.yh, 1, HB], r4, p.own)
    net.send(W.at[p.x, :, :, HB], W.at[p.x, :, :, HB], x1, p.at(x=p.xp))
    net.send(W.at[p.x, :, :, HB], W.at[p.x, :, :, HB], x2, p.at(x=p.xm))
    yield
    net.got(W.at[p.xm, :, :, HB], x1)
    net.send(W.at[p.xm, :, 0, HB], W.at[p.xm, :, 0, HB], x3, p.at(x=p.xp))
    net.got(W.at[p.xp, :, :, HB], x2)
    net.send(W.at[p.xp, :, 1, HB], W.at[p.xp, :, 1, HB], x4, p.at(x=p.xm))
    net.got(W.at[:, p.yhm, :, HA], y1, p.opp)
    net.send(W.at[:, p.yhm, 0, HA], W.at[:, p.yhm, 0, HA], y3, p.at(y=p.yp), p.opp)
    net.got(W.at[:, p.yhp, :, HA], y2, p.opp)
    net.send(W.at[:, p.yhp, 1, HA], W.at[:, p.yhp, 1, HA], y4, p.at(y=p.ym), p.opp)
    yield
    net.got(W.at[:, 1 - p.yh, 0, HA], y3, p.own)
    net.got(W.at[:, 1 - p.yh, 1, HA], y4, p.own)
    net.got(W.at[p.x2, :, 0, HB], x3)
    net.got(W.at[p.x2, :, 1, HB], x4)


def gather_ring(net, a, out):
    p = net.p
    s1, s3, s2 = net.sem(), net.sem(), net.sem()
    k = net.sem(4)
    net.send(a, out.at[p.z, p.c], s1, p.at(z=p.zf))
    net.send(a, out.at[p.z, p.c], s3, p.at(z=p.zb))
    net.send(a, out.at[p.z, p.c], k + 0, p.at(c=p.o))
    yield
    net.got(out.at[p.z, p.o], k + 0)
    yield
    jf, jb = (p.zf - p.z + 4) % 4, (p.zb - p.z + 4) % 4
    net.got(out.at[p.zb, p.c], s1)
    net.send(out.at[p.zb, p.c], out.at[p.zb, p.c], s2, p.at(z=p.zf))
    net.send(out.at[p.zb, p.c], out.at[p.zb, p.c], k + jb, p.at(c=p.o))
    net.got(out.at[p.zf, p.c], s3)
    net.send(out.at[p.zf, p.c], out.at[p.zf, p.c], k + jf, p.at(c=p.o))
    yield
    net.got(out.at[p.zp, p.o], k + 1)
    net.got(out.at[p.zm, p.o], k + 3)
    yield
    net.got(out.at[p.z2, p.c], s2)
    net.send(out.at[p.z2, p.c], out.at[p.z2, p.c], k + 2, p.at(c=p.o))
    net.got(out.at[p.z2, p.o], k + 2)


class ReduceRing:
    def __init__(self, net, V, out, RC, SB, RZ):
        self.net, self.V, self.out, self.RC, self.SB, self.RZ = net, V, out, RC, SB, RZ
        self.s2, self.sd, self.sr, self.k = net.sem(), net.sem(), net.sem(), net.sem(4)

    def push(self, j):
        p = self.net.p
        self.net.send(self.V.at[(p.z + j) % 4, p.o], self.RC.at[j], self.k + j, p.at(c=p.o))

    def rest(self):
        net, p, V, RC, SB, RZ, k = self.net, self.net.p, self.V, self.RC, self.SB, self.RZ, self.k
        jf, jb = (p.zf - p.z + 4) % 4, (p.zb - p.z + 4) % 4
        net.got(RC.at[2], k + 2)
        add(SB.at[0], V.at[p.z2, p.c], RC.at[2])
        net.send(SB.at[0], RZ.at[0], self.s2, p.at(z=p.zf))
        yield
        net.got(RC.at[jb], k + jb)
        add(SB.at[1], V.at[p.zb, p.c], RC.at[jb])
        net.send(SB.at[1], RZ.at[1], self.sd, p.at(z=p.zb))
        net.got(RC.at[jf], k + jf)
        add(RC.at[jf], V.at[p.zf, p.c], RC.at[jf])
        yield
        net.got(RZ.at[0], self.s2)
        add(RC.at[jf], RC.at[jf], RZ.at[0])
        net.send(RC.at[jf], RZ.at[2], self.sr, p.at(z=p.zf))
        net.got(RC.at[0], k + 0)
        add(RC.at[0], V.at[p.z, p.c], RC.at[0])
        yield
        net.got(RZ.at[1], self.sd)
        net.got(RZ.at[2], self.sr)
        add(self.out, RC.at[0], RZ.at[1], RZ.at[2])


def step(job, times=1):
    for _ in range(times):
        next(job, None)


def dot(a, b, dims):
    return lax.dot_general(a, b, (dims, ((), ())), preferred_element_type=F32)


NN, NT, TN = ((1,), (0,)), ((1,), (1,)), ((0,), (0,))


def whole(ref, columns=slice(None)):
    v = ref[:, :, :, :, columns]
    return v.reshape(D, v.shape[-1])


def row_norm(src, dst, gain, rows=32):
    def one(i, _):
        at = pl.ds(pl.multiple_of(i * rows, rows), rows)
        v = src[at].astype(F32)
        inv = lax.rsqrt(jnp.mean(v * v, axis=1, keepdims=True) + epsilon)
        dst[at] = (v * inv * gain).astype(dst.dtype)

    lax.fori_loop(0, ROWS // rows, one, None)


def forward_kernel(*refs):
    (tok, gout, conv_s, gu_s, down_s, small_s,
     n1_o, n2_o, go_o, ggu_o, hid_o, b_o, c_o, v_o, bx_o, mx_o, wc_o, pg_o, pf_o, resid, gains,
     T1, N1, GO, N2, WC, WG, WD, SM, B, C, V, BX, MX, GA, HID, GGU, PA, PB, PF, RC, SB, RZ,
     send, recv, local) = refs
    p = Place()
    BX[0, :, 0:8] = jnp.zeros((2, 8, 256), F32)
    greet(p, True, True)
    net = Net(p, send, recv, local)
    block = lambda j: (p.z + j) % 4
    halo = net.sem()

    gt = gather_ring(net, tok, T1)
    ac = gather_plane(net, conv_s, WC)
    am = gather_plane(net, small_s, SM)
    ad = gather_plane(net, down_s, WD)
    au = gather_plane(net, gu_s.at[:, 0:GA_N], WG.at[:, :, :, :, 0:GA_N])
    av = gather_plane(net, gu_s.at[:, GA_N:], WG.at[:, :, :, :, GA_N:])
    go = gather_ring(net, gout, GO)
    outs = []

    step(ac), step(am), step(gt)
    own_tok = net.copy(tok, T1.at[p.z, p.c])
    own_gout = net.copy(gout, GO.at[p.z, p.c])
    step(am), step(ac)
    step(am), step(ac)
    step(ad), step(au)
    step(am), step(ac)
    step(ad), step(au)
    step(gt, 2)
    step(go)
    step(am), step(ac)
    gains[...] = jnp.zeros(gains.shape, F32)
    for s in range(16):
        piece = SM[s // 4, (s // 2) % 2, s % 2, 0:16].astype(F32)
        at = (96 * s) // 128 * 128
        n = min(256, gains.shape[1] - at)
        gains[0:16, at : at + n] = gains[0:16, at : at + n] + piece[:, :n]
    gains[16:32, 0:256] = SM[0, 0, 0, 16:32].astype(F32)
    g_mix, g_ffn = gains[0:1, :D], gains[1:2, :D]
    taps = [gains[16 + i : 17 + i, 0:256] for i in range(3)]

    own_tok()
    lanes = lax.broadcasted_iota(jnp.int32, (256, 128), 1) < 64

    def project(j):
        zj = block(j)
        for cc in range(2):
            row_norm(T1.at[zj, cc], N1.at[zj, cc], g_mix)
        r = dot(N1[zj].reshape(256, D), whole(WC), NN)
        b1 = jnp.where(lanes, r[:, 512:640], 0.0)
        c1 = jnp.where(lanes, pltpu.roll(r[:, 512:640], 64, 1), 0.0)
        v1 = jnp.where(lanes, pltpu.roll(r[:, 640:768], 64, 1), 0.0)
        b = jnp.concatenate([r[:, 0:128], b1], axis=1)
        v = jnp.concatenate([r[:, 256:384], v1], axis=1)
        B[zj] = b.reshape(2, 128, 256)
        V[zj] = v.reshape(2, 128, 256)
        C[zj] = jnp.concatenate([r[:, 128:256], c1], axis=1).reshape(2, 128, 256)
        BX[zj, :, 8:136] = (b * v).reshape(2, 128, 256)

    project(0)
    step(ad), step(au)
    step(gt)
    project(1)
    project(3)
    step(gt)
    project(2)
    net.send(BX.at[0:4, :, 128:136], BX.at[pl.ds(p.yl, 4), :, 0:8], halo, p.at(y=p.y + 1 - 2 * p.yl))
    step(go, 2)
    step(av)
    net.got(BX.at[pl.ds(1 - p.yl, 4), :, 0:8], halo)

    r1 = ReduceRing(net, PA, resid, RC, SB, RZ)

    def mix(j):
        zj = block(j)
        for cc in range(2):
            conv = (
                taps[0] * BX[zj, cc, 8:136] + taps[1] * BX[zj, cc, 7:135] + taps[2] * BX[zj, cc, 6:134]
            )
            MX[zj, cc] = (C[zj, cc] * conv).astype(BF)
        o = jnp.concatenate([whole(WC, slice(384, 512)), whole(WC, slice(640, 768))], axis=1)
        PA[zj] = dot(MX[zj].reshape(256, 256), o, NT).astype(BF).reshape(2, 128, D)
        r1.push(j)

    for j in (2, 1, 3, 0):
        mix(j)
    r1 = r1.rest()
    step(r1)
    step(ad), step(au), step(av)
    step(r1)
    step(go, 2)
    step(ad), step(au), step(av)
    step(r1)
    step(av)
    own_gout()

    def act(j):
        zj = block(j)
        GA[zj] = dot(GO[zj].reshape(256, D), whole(WD), NN)

    act(0)
    step(r1)

    def second(i, _):
        at = pl.ds(pl.multiple_of(i * 32, 32), 32)
        v = tok[at].astype(F32) + resid[at]
        resid[at] = v
        inv = lax.rsqrt(jnp.mean(v * v, axis=1, keepdims=True) + epsilon)
        N2[p.z, p.c, at] = (v * inv * g_ffn).astype(BF)

    lax.fori_loop(0, ROWS // 32, second, None)
    g2 = gather_ring(net, N2.at[p.z, p.c], N2)
    step(g2)
    step(av)
    outs.append(net.copy(N1, n1_o))
    outs.append(net.copy(B, b_o))
    outs.append(net.copy(C, c_o))
    outs.append(net.copy(V, v_o))
    outs.append(net.copy(BX.at[0:4], bx_o))
    outs.append(net.copy(MX, mx_o))
    outs.append(net.copy(WC, wc_o))
    outs.append(net.copy(GO, go_o))
    step(g2)

    def feed(j):
        zj = block(j)
        n2 = N2[zj].reshape(256, D)
        for t in range(7):
            r = dot(n2, whole(WG, slice(256 * t, 256 * t + 256)), NN)
            g, u = r[:, :128], r[:, 128:]
            ga = GA[zj, :, 128 * t : 128 * t + 128]
            s = jax.nn.sigmoid(g)
            silu = g * s
            HID[zj, :, 128 * t : 128 * t + 128] = (silu * u).astype(BF)
            GGU[zj, :, 256 * t : 256 * t + 128] = (ga * u * s * (1.0 + g * (1.0 - s))).astype(BF)
            GGU[zj, :, 256 * t + 128 : 256 * t + 256] = (ga * silu).astype(BF)

    def back(j):
        zj = block(j)
        PB[zj] = dot(GGU[zj], whole(WG), NT).astype(BF).reshape(2, 128, D)

    def down(j):
        zj = block(j)
        PF[zj] = dot(HID[zj], whole(WD), NT).astype(BF).reshape(2, 128, D)

    feed(0)
    act(1)
    step(g2)
    back(0)
    act(3)
    act(2)
    step(g2)
    feed(1)
    back(1)
    feed(3)
    back(3)
    step(g2)
    outs.append(net.copy(N2, n2_o))
    feed(2)
    back(2)
    outs.append(net.copy(PB, pg_o))
    outs.append(net.copy(HID, hid_o))
    outs.append(net.copy(GGU, ggu_o))
    for j in range(4):
        down(j)
    outs.append(net.copy(PF, pf_o))
    for job in (gt, go, g2, ac, am, ad, au, av):
        assert next(job, "end") == "end"
    net.finish()
    for done in outs:
        done()


GA_N = 1024


def forward_call(tok, gout, conv_pack, gu_pack, down_pack, small):
    any_, vm = pl.BlockSpec(memory_space=pl.ANY), pl.BlockSpec(memory_space=pltpu.VMEM)
    ring = (4, 2, ROWS, D)
    outs = [shape(ring), shape(ring), shape(ring), shape((4, 256, 1792)), shape((4, 256, FP))]
    outs += [shape((4, 2, ROWS, 256), F32)] * 3 + [shape((4, 2, 136, 256), F32), shape((4, 2, ROWS, 256))]
    outs += [slots(768), shape(ring), shape(ring), shape((ROWS, D), F32), shape((32, D), F32)]
    vmem = lambda s, t=BF: pltpu.VMEM(s, t)
    scratch = [vmem(ring)] * 4 + [vmem((4, 2, 2, 96, n)) for n in (768, 1792, FP)]
    scratch += [vmem((4, 2, 2, 32, 256))] + [vmem((4, 2, ROWS, 256), F32)] * 3
    scratch += [vmem((5, 2, 136, 256), F32), vmem((4, 2, ROWS, 256)), vmem((4, 256, FP), F32)]
    scratch += [vmem((4, 256, FP)), vmem((4, 256, 1792)), vmem(ring), vmem(ring), vmem(ring)]
    scratch += [vmem((4, ROWS, D)), vmem((2, ROWS, D)), vmem((3, ROWS, D))]
    scratch += [pltpu.SemaphoreType.DMA((160,)), pltpu.SemaphoreType.DMA((160,)), pltpu.SemaphoreType.DMA((24,))]
    return pl.pallas_call(
        forward_kernel,
        out_shape=tuple(outs),
        in_specs=[vm] + [any_] * 5,
        out_specs=tuple([any_] * 13 + [vm] * 2),
        scratch_shapes=scratch,
        compiler_params=pltpu.CompilerParams(
            collective_id=0, has_side_effects=True, vmem_limit_bytes=VMEM_LIMIT),
        name="forward",
    )(tok, gout, conv_pack, gu_pack, down_pack, small)


def exchange(name, number, gathers=(), rings=(), ring_sums=(), plane_sums=()):
    ng, nz, ns, nq = len(gathers), len(rings), len(ring_sums), len(plane_sums)

    def kernel(*refs):
        refs = list(refs)

        def take(n):
            part, refs[:] = refs[:n], refs[n:]
            return part

        a, b, d, e = take(ng), take(nz), take(ns), take(nq)
        ao, bo, do, eo = take(ng), take(nz), take(ns), take(nq)
        ds = [take(3) for _ in range(ns)]
        es = [take(8) for _ in range(nq)]
        send, recv, local = refs
        p = Place()
        greet(p, bool(ng + nq), bool(nz + ns))
        net = Net(p, send, recv, local)
        rr = [ReduceRing(net, v, o, *s) for v, o, s in zip(d, do, ds)]
        for r in rr:
            for j in (2, 1, 3, 0):
                r.push(j)
        jobs = [r.rest() for r in rr]
        jobs += [gather_ring(net, v, o) for v, o in zip(b, bo)]
        dones = [net.copy(v, o.at[p.z, p.c]) for v, o in zip(b, bo)]
        jobs += [gather_plane(net, v, o) for v, o in zip(a, ao)]
        jobs += [reduce_plane(net, v, o, *s) for v, o, s in zip(e, eo, es)]
        together(*jobs)
        net.finish()
        for f in dones:
            f()

    any_, vm = pl.BlockSpec(memory_space=pl.ANY), pl.BlockSpec(memory_space=pltpu.VMEM)
    scratch = []
    for v in ring_sums:
        scratch += ring_scratch(v.shape[-1])
    for v in plane_sums:
        scratch += plane_scratch(v.shape[-1])
    count = 24 * (ng + nq) + 12 * (nz + ns)
    scratch += [pltpu.SemaphoreType.DMA((count,))] * 2 + [pltpu.SemaphoreType.DMA((ng + nz + 1,))]
    outs = [slots(v.shape[-1]) for v in gathers] + [blocks(v.shape[-1]) for v in rings]
    outs += [shape((ROWS, v.shape[-1]), F32) for v in ring_sums]
    outs += [shape((96, v.shape[-1]), F32) for v in plane_sums]
    return pl.pallas_call(
        kernel,
        out_shape=tuple(outs),
        in_specs=[any_] * (ng + nz) + [vm] * (ns + nq),
        out_specs=tuple([any_] * (ng + nz) + [vm] * (ns + nq)),
        scratch_shapes=scratch,
        compiler_params=pltpu.CompilerParams(
            collective_id=number, has_side_effects=True, vmem_limit_bytes=VMEM_LIMIT),
        name=name,
    )(*gathers, *rings, *ring_sums, *plane_sums)


def norm_backward_rule(gradient_of_normalized, centered_input, inverse_root, gain_widened):
    weighted_rows = gain_widened * gradient_of_normalized
    return inverse_root * (
        weighted_rows
        - centered_input * jnp.mean(weighted_rows * centered_input, axis=1, keepdims=True)
    )


SWAP = [(t, t ^ 1) for t in range(8)]


def matmul(a, b, dims, out=F32):
    return lax.dot_general(a, b, (dims, ((), ())), preferred_element_type=F32).astype(out)


def per_device(tokens, gain_mix, in_weight, conv_kernel, out_weight, gain_ffn, gate_weight, up_weight, down_weight, lengths, cotangent):
    dp, t = lax.axis_index("dp"), lax.axis_index("tensor")
    z, yl, c = t // 2, t % 2, dp % 2
    position = t * ROWS + jnp.arange(ROWS)
    live = (position < lengths[0]).astype(F32)[:, None]

    b, cg, v = in_weight[:, 0], in_weight[:, 1], in_weight[:, 2]
    o = out_weight.T
    conv_pack = jnp.concatenate(
        [b[:, :128], cg[:, :128], v[:, :128], o[:, :128], b[:, 128:], cg[:, 128:], o[:, 128:], v[:, 128:]],
        axis=1,
    )
    wide = lambda w: jnp.pad(w, ((0, 0), (0, FP - FB)))
    gu_pack = jnp.stack([wide(gate_weight).reshape(96, 7, 128), wide(up_weight).reshape(96, 7, 128)], axis=2)
    gu_pack = gu_pack.reshape(96, 1792)
    down_pack = wide(down_weight.T)
    small = jnp.zeros((32, 256), BF)
    off = (96 * dp) % 128
    small = lax.dynamic_update_slice(small, jnp.stack([gain_mix, gain_ffn]), (0, off))
    small = lax.dynamic_update_slice(small, conv_kernel, (16, 0))
    grad_out = (live * cotangent.astype(F32)).astype(BF)

    (normed_all, normed2_all, gout_all, ggu, hidden, bv, cv, vv, bxv, mixed, wc, gn2, ffn_part, resid, gains) = (
        forward_call(tokens, grad_out, conv_pack, gu_pack, down_pack, small)
    )
    g_mix, g_ffn = gains[0], gains[1]
    taps = gains[16:19, :CH]
    tok = tokens.astype(F32)
    inv2 = lax.rsqrt(jnp.mean(resid * resid, axis=1, keepdims=True) + epsilon)
    xhat2 = resid * inv2
    flat = lambda a: a.reshape(1024, -1)
    normed_all, normed2_all, gout_all = flat(normed_all), flat(normed2_all), flat(gout_all)
    ggu, hidden, mixed = flat(ggu), flat(hidden), flat(mixed)[:, :CH]
    wc = wc.reshape(D, 768)
    w_in = jnp.concatenate([wc[:, 0:128], wc[:, 512:576], wc[:, 128:256], wc[:, 576:640], wc[:, 256:384], wc[:, 704:768]], axis=1)
    w_out_t = jnp.concatenate([wc[:, 384:512], wc[:, 640:704]], axis=1)
    c_gate, value, b_gate = flat(cv)[:, :CH], flat(vv)[:, :CH], flat(bv)[:, :CH]
    bx = flat(bxv[:, :, 8:136])[:, :CH]
    bx_one = flat(bxv[:, :, 7:135])[:, :CH]
    bx_two = flat(bxv[:, :, 6:134])[:, :CH]
    conv_sum = taps[0] * bx + taps[1] * bx_one + taps[2] * bx_two
    gu_full = matmul(normed2_all, ggu, ((0,), (0,)), BF).reshape(D, 7, 2, 128)
    gate_full, up_full = gu_full[:, :, 0].reshape(D, FP), gu_full[:, :, 1].reshape(D, FP)
    down_full = matmul(gout_all, hidden, ((0,), (0,)), BF)

    as_slots = lambda v: v.reshape(4, 2, 2, 96, v.shape[-1])
    gn2_rows, gate_sum = exchange(
        "fourth", 3, ring_sums=(gn2,), plane_sums=(as_slots(gate_full),)
    )
    grad_resid = grad_out.astype(F32) + norm_backward_rule(gn2_rows, xhat2, inv2, g_ffn)
    branch_all, up_sum = exchange(
        "fifth", 4, rings=(grad_resid.astype(BF),), plane_sums=(as_slots(up_full),)
    )
    branch_all = branch_all.reshape(1024, D)
    out_full = matmul(branch_all, mixed, ((0,), (0,)), BF)
    grad_mixed = matmul(branch_all, w_out_t, ((1,), (0,)))
    grad_c = grad_mixed * conv_sum
    grad_conv = grad_mixed * c_gate
    gc4 = grad_conv.reshape(4, 2, ROWS, CH)
    ahead = lax.ppermute(gc4[:, :, :2], "tensor", SWAP)
    shifted = jnp.pad(ahead, ((0, 1), (0, 0), (0, 0), (0, 0)))[1:]
    ahead = jnp.where(yl == 0, ahead, shifted)
    ext = jnp.concatenate([gc4, ahead], axis=2)
    grad_bx = (
        taps[0] * grad_conv
        + taps[1] * ext[:, :, 1:-1].reshape(1024, CH)
        + taps[2] * ext[:, :, 2:].reshape(1024, CH)
    )
    kernel_part = jnp.stack(
        [jnp.sum(grad_conv * bx, 0), jnp.sum(grad_conv * bx_one, 0), jnp.sum(grad_conv * bx_two, 0)]
    )
    grad_projected = jnp.concatenate([grad_bx * value, grad_c, grad_bx * b_gate], axis=1).astype(BF)
    in_full = matmul(normed_all, grad_projected, ((0,), (0,)), BF)
    gn1 = matmul(grad_projected, w_in, ((1,), (1,)), BF)
    conv_full = jnp.concatenate([in_full, out_full], axis=1)
    taps_at = jnp.pad(kernel_part.T.reshape(16, 12, 3), ((0, 0), (0, 84), (0, 0))).astype(BF)
    down_full = lax.dynamic_update_slice(down_full, taps_at.reshape(D, 3), (0, FB))
    gn1_rows, ffn_rows, down_sum, conv_sums = exchange(
        "sixth",
        5,
        ring_sums=(gn1.reshape(4, 2, ROWS, D), ffn_part),
        plane_sums=(as_slots(down_full), as_slots(conv_full)),
    )
    layer_out = (live * (resid + ffn_rows)).astype(BF)
    inv1 = lax.rsqrt(jnp.mean(tok * tok, axis=1, keepdims=True) + epsilon)
    tokens_grad = (grad_resid + norm_backward_rule(gn1_rows, tok * inv1, inv1, g_mix)).astype(BF)

    in_grad = conv_sums[:, : 3 * CH].reshape(96, 3, CH)
    out_grad = conv_sums[:, 3 * CH :].T
    gate_grad, up_grad = gate_sum[:, :FB], up_sum[:, :FB]
    down_grad = down_sum[:, :FB].T
    mix_share = jnp.sum(in_grad * in_weight.astype(F32), axis=(1, 2)) / gain_mix.astype(F32)
    ffn_share = jnp.sum(
        gate_grad * gate_weight.astype(F32) + up_grad * up_weight.astype(F32), axis=1
    ) / gain_ffn.astype(F32)
    shares = lax.psum_scatter(
        jnp.stack([mix_share, ffn_share]).reshape(2, 8, 12), "tensor", scatter_dimension=1
    )
    move = [(i, (i % 8) * 16 + i // 8) for i in range(128)]
    kernel_grad = lax.ppermute(down_sum[:12, FB : FB + 3].T, ("dp", "tensor"), move)
    return (
        layer_out,
        tokens_grad,
        shares[0],
        in_grad,
        kernel_grad,
        out_grad,
        shares[1],
        gate_grad,
        up_grad,
        down_grad,
    )


def solution(mesh):
    placed = (
        P(("dp", "tensor"), None),
        P("dp"),
        P("dp", None, "tensor"),
        P(None, "tensor"),
        P("tensor", "dp"),
        P("dp"),
        P("dp", "tensor"),
        P("dp", "tensor"),
        P("tensor", "dp"),
        P("dp"),
        P(("dp", "tensor"), None),
    )
    return jax.shard_map(
        per_device,
        mesh=mesh,
        in_specs=placed,
        out_specs=(
            P(("dp", "tensor"), None),
            P(("dp", "tensor"), None),
            P(("dp", "tensor")),
            P("dp", None, "tensor"),
            P(None, ("dp", "tensor")),
            P("tensor", "dp"),
            P(("dp", "tensor")),
            P("dp", "tensor"),
            P("dp", "tensor"),
            P("tensor", "dp"),
        ),
        check_vma=False,
    )
```

time: 450 us -> 448 us (level)
  local copies, waits for them, and re-layouts: 62.8 us -> 133 us
  matrix products: 63.3 us -> 32.7 us
  Pallas kernels: 242 us -> 220 us
  other arithmetic: 41.5 us -> 23.9 us
    pallas_call x6 -> x3, Pallas kernels: 242 us -> 109 us  [exchange(): pl.pallas_call(kernel, out_shape=tuple(outs), in_specs=[any_] * (ng + nz)...]
    pallas_call x0 -> x1, Pallas kernels: none -> 111 us  [forward_call(): pl.pallas_call(forward_kernel, out_shape=tuple(outs), in_specs=[vm] + [an...]
    slice x3 -> x13, local copies, waits for them, and re-layouts: 3.59 us -> 44.6 us  [the longest x1 37.4 us: per_device(): gu_full[:, :, 1].reshape(D, FP)]
    dot_general x15 -> x6, matrix products: 63.3 us -> 32.7 us  [matmul(): lax.dot_general(a, b, (dims, ((), ())), preferred_element_type=F32)]
    another operation x0 -> x5, local copies, waits for them, and re-layouts: none -> 13.8 us  [the longest x2 12.9 us: per_device(): as_slots = lambda v: v.reshape(4, 2, 2, 96, v.shape[-1])]
    unnamed x89 -> x81, local copies, waits for them, and re-layouts: 15.3 us -> 23.7 us
    convert_element_type x5 -> x0, other arithmetic: 5.8 us -> none  [the longest x1 2.3 us: per_device(): mixed = (c_gate * conv_sum).astype(BF)]
    concatenate x2, local copies, waits for them, and re-layouts: 0.11 us -> 5.64 us  [the longest x1 4.87 us: per_device(): jnp.concatenate([wc[:, 0:128], wc[:, 512:576], wc[:, 128:256], wc[:, 576:...]
  transfers between devices with their start and end apart: 3 -> 2, of which waited for: 1 -> 1; matrix products, arithmetic and copies ran while one was open for 5% -> 8% of each run, Pallas kernels for 0% -> 0%
where the time goes in v2:
time: 448 us; the launch traced here: 439 us
  Pallas kernels  220 us (49%)
  local copies, waits for them, and re-layouts  133 us (30%)
  matrix products  32.7 us (7%)
  other arithmetic  23.9 us (5%)
  blocking collectives  19.6 us (4%)
  waiting for transfers between devices  4.9 us (1%)
    pallas_call x1, Pallas kernels, forward_call(): pl.pallas_call(forward_kernel, out_shape=tuple(outs), in_specs=[vm] + [an...  111 us
    pallas_call x3, Pallas kernels, exchange(): pl.pallas_call(kernel, out_shape=tuple(outs), in_specs=[any_] * (ng + nz)...  109 us
    slice x1, local copies, waits for them, and re-layouts, per_device(): gu_full[:, :, 1].reshape(D, FP)  37.4 us
    dot_general x6, matrix products, matmul(): lax.dot_general(a, b, (dims, ((), ())), preferred_element_type=F32)  32.7 us
    unnamed x81, local copies, waits for them, and re-layouts  23.7 us
    unnamed x1, blocking collectives  19.6 us
    another operation x2, local copies, waits for them, and re-layouts, per_device(): as_slots = lambda v: v.reshape(4, 2, 2, 96, v.shape[-1])  12.9 us
    reshape x1, local copies, waits for them, and re-layouts, per_device(): gu_full = matmul(normed2_all, ggu, ((0,), (0,)), BF).reshape(D, 7, 2, 128)  11 us
  transfers between devices with their start and end apart: 2, of which 1 were waited for; matrix products, arithmetic and copies ran while one was open for 8% of the time, Pallas kernels for 0%

profile of v2, /device:TPU:30, one launch (start us, length us, event | category | flops | bytes accessed | tf_op | source)
XLA Modules:
  0.0 439.5 jit_solution(14705611716026405210)
XLA Ops:
  10.6 111.0 %forward.1 = (bf16[4,2,128,1536]{3,2,1,0:T(8,128)(2,1)}, bf16[4,2,128,1536]{3,2,1,0:T(8,128)(2,1)}, bf16[4,2,128,1536]{3,2,1,0:T(8,128)(2,1)}, bf16[4,256,1792]{...) custom-call(bf16[128,1536]{1,0:T(8,128)(2,1)} %refs_0_.1, ...), custom_call_target="tpu_custom_call" | custom-call | tf_op jit(solution)/shard_map/forward/pallas_call | solution.py:610
  121.6 2.7 fusion.19
  124.3 1.5 fusion.20
  126.7 1.4 fusion.22
  128.1 10.5 %convolution_convert_fusion = bf16[1536,1792]{1,0:T(8,128)(2,1)} fusion(bf16[1024,1536]{1,0:T(8,128)(2,1)} %bitcast.99, bf16[1024,1792]{1,0:T(8,128)(2,1)S(1)} %bitcast.96), kind=kOutput, calls=%fused_computation | convolution fusion | flops 5639897088 | bytes 12320768 | tf_op jit(solution)/shard_map/dot_general | solution.py:689
  138.6 11.0 %reshape.138 = bf16[1536,7,2,128]{3,2,1,0:T(2,128)(2,1)} reshape(bf16[1536,1792]{1,0:T(8,128)(2,1)} %convolution_convert_fusion) | data formatting | bytes 11010048 | tf_op jit(solution)/shard_map/reshape | solution.py:733
  149.6 37.4 %slice_reduce_fusion = (bf16[1536,7,128]{2,1,0:T(8,128)(2,1)}, bf16[1536,7,128]{2,1,0:T(8,128)(2,1)}) fusion(bf16[1536,7,2,128]{3,2,1,0:T(2,128)(2,1)} %reshape.138), kind=kLoop, calls=%fused_computation.1 | loop fusion | bytes 11010048 | tf_op jit(solution)/shard_map/slice | solution.py:734
  187.0 6.4 %reshape_reshape_squeeze.6.refs_1_ = bf16[4,2,2,96,896]{4,3,2,1,0:T(8,128)(2,1)} reshape(bf16[1536,7,128]{2,1,0:T(8,128)(2,1)} %get-tuple-element.87) | data formatting | bytes 5505024 | tf_op jit(solution)/shard_map/reshape;reshape;squeeze | solution.py:737
  193.6 32.9 %fourth.1 = (f32[128,1536]{1,0:T(8,128)}, f32[96,896]{1,0:T(8,128)}) custom-call(bf16[4,2,128,1536]{3,2,1,0:T(8,128)(2,1)} %get-tuple-element.35.refs_0_, bf16[4,2,2,96,896]{4,3,2,1,0:T(8,128)(2,1)} %reshape_reshape_squeeze.6.refs_1_), custom_call_target="tpu_custom_call" | custom-call | tf_op jit(solution)/shard_map/fourth/pallas_call | solution.py:665
  227.0 1.4 multiply_reduce_fusion.3
  228.4 2.2 fusion.18.refs_0_
  230.6 6.5 %reshape_reshape_squeeze.7.refs_1_ = bf16[4,2,2,96,896]{4,3,2,1,0:T(8,128)(2,1)} reshape(bf16[1536,7,128]{2,1,0:T(8,128)(2,1)} %get-tuple-element.86) | data formatting | bytes 5505024 | tf_op jit(solution)/shard_map/reshape;reshape;squeeze | solution.py:737
  237.0 1.6 fusion.21
  238.6 2.5 copy.79
  241.1 2.5 copy.80
  244.8 2.6 copy.76
  247.3 30.6 %fifth.1 = (bf16[4,2,128,1536]{3,2,1,0:T(8,128)(2,1)}, f32[96,896]{1,0:T(8,128)}) custom-call(bf16[128,1536]{1,0:T(8,128)(2,1)} %fusion.18.refs_0_, bf16[4,2,2,96,896]{4,3,2,1,0:T(8,128)(2,1)} %reshape_reshape_squeeze.7.refs_1_), custom_call_target="tpu_custom_call" | custom-call | tf_op jit(solution)/shard_map/fifth/pallas_call | solution.py:665
  278.0 5.3 %multiply_reduce_fusion.2 = (bf16[192]{0:T(256)(128)(2,1)}, bf16[192]{0:T(256)(128)(2,1)}, bf16[192]{0:T(256)(128)(2,1)}, f32[1024,192]{0,1:T(8,128)S(1)}, bf16[1024,192]{0,1:T(8,128)(2,1)}) fusion(f32[1024,192]{0,1:T(8,128)S(1)} %copy-done.9, f32[1024,192]{0,1:T(8,128)} %copy.81, f32[1024,192]{0,1:T(8,128)S(1)} %copy-done.10, f32[1024,192]{0,1:T(8,128)} %copy.76, ...), kind=kOutput, calls=%fused_computation.30 | convolution fusion | flops 607911360 | bytes 8064384 | tf_op jit(solution)/shard_map/dot_general | solution.py:689
  283.9 1.4 copy.77
  285.2 1.4 collective-permute-start
  286.7 2.3 add_reduce_fusion
  289.0 3.7 convolution_convert_fusion.4
  292.8 5.1 %convolution_convert_fusion.2 = bf16[1536,896]{1,0:T(8,128)(2,1)} fusion(bf16[1024,1536]{1,0:T(8,128)(2,1)S(1)} %bitcast.98, bf16[1024,896]{1,0:T(8,128)(2,1)S(1)} %bitcast.100), kind=kOutput, calls=%fused_computation.4 | convolution fusion | flops 2819948544 | bytes 7733248 | tf_op jit(solution)/shard_map/dot_general | solution.py:689
  299.9 2.4 copy.78
  302.4 1.5 copy.82
  303.9 1.4 reshape.153
  305.3 1.5 copy.83
  306.8 1.6 pad.23.clone
  309.7 4.7 %dynamic_update_slice.11 = bf16[1536,896]{1,0:T(8,128)(2,1)} dynamic-update-slice(bf16[1536,896]{1,0:T(8,128)(2,1)} %convolution_convert_fusion.2, bf16[1536,3]{1,0:T(8,128)(2,1)} %bitcast.83, s32[]{:T(128)} %constant.43.clone.1, s32[]{:T(128)} %constant.55.clone.1) | dynamic-update-slice | bytes 18436 | tf_op jit(solution)/shard_map/dynamic_update_slice | solution.py:768
  314.5 4.9 %concatenate.24 = bf16[1536,576]{1,0:T(8,128)(2,1)} concatenate(bf16[1536,128]{1,0:T(8,128)(2,1)} %get-tuple-element.103, bf16[1536,64]{1,0:T(8,128)(2,1)} %get-tuple-element.107, bf16[1536,128]{1,0:T(8,128)(2,1)} %get-tuple-element.102, bf16[1536,64]{1,0:T(8,128)(2,1)} %get-tuple-element.106, bf16[1536,128]{1,0:T(8,128)(2,1)} %get-tuple-element.101, ...), dimensions={1} | concatenate | bytes 3538944 | tf_op jit(solution)/shard_map/concatenate | solution.py:726
  319.3 1.4 fusion.14
  320.7 1.9 copy.60
  322.6 5.9 %fusion.8 = (f32[4,2,128,192]{2,1,0,3:T(2,128)}, f32[4,2,128,192]{2,1,0,3:T(2,128)}) fusion(f32[4,2,128,192]{2,1,0,3:T(2,128)S(1)} %reshape.142, f32[4,2,2,192]{2,1,0,3:T(2,128)} %copy.60), kind=kLoop, calls=%fused_computation.21 | loop fusion | flops 393216 | bytes 2371584 | tf_op jit(solution)/shard_map/concatenate | solution.py:754
  328.5 2.7 reshape.143
  331.2 2.7 reshape.144
  333.9 1.8 multiply_convert_fusion.3
  336.6 2.0 convolution_convert_fusion.3
  338.7 2.7 copy.67
  341.4 6.2 %convolution_convert_fusion.1 = bf16[1024,1536]{1,0:T(8,128)(2,1)} fusion(bf16[1536,576]{1,0:T(8,128)(2,1)} %concatenate.24, bf16[1024,192]{0,1:T(8,128)(2,1)} %copy-done.14, bf16[1024,192]{0,1:T(8,128)(2,1)} %get-tuple-element.99, bf16[1024,192]{0,1:T(8,128)(2,1)} %copy-done.13), kind=kOutput, calls=%fused_computation.3 | convolution fusion | flops 1817051136 | bytes 6094848 | tf_op jit(solution)/shard_map/dot_general | solution.py:689
  347.6 45.1 %sixth.1 = (f32[128,1536]{1,0:T(8,128)}, f32[128,1536]{1,0:T(8,128)}, f32[96,896]{1,0:T(8,128)}, f32[96,768]{1,0:T(8,128)}) custom-call(bf16[4,2,128,1536]{3,2,1,0:T(8,128)(2,1)} %bitcast.79, bf16[4,2,128,1536]{3,2,1,0:T(8,128)(2,1)} %get-tuple-element.45.refs_1_, bf16[4,2,2,96,896]{4,3,2,1,0:T(8,128)(2,1)} %bitcast.80, bf16[4,2,2,96,768]{4,3,2,1,0:T(8,128)(2,1)} %bitcast.70), custom_call_target="tpu_custom_call" | custom-call | tf_op jit(solution)/shard_map/sixth/pallas_call | solution.py:665
  392.8 1.8 slice.193
  395.6 1.7 slice_bitcast_fusion
  397.3 1.4 slice_bitcast_fusion.5
  404.6 19.6 %all-reduce.5 = f32[2,8,12]{2,0,1:T(2,128)} all-reduce(f32[2,8,12]{2,0,1:T(2,128)} %copy.70), channel_id=2, replica_groups=mesh['dp'=16,'tensor'=8] {'tensor'}, use_global_device_ids=true, to_apply=%region_9.10.clone | all-reduce | flops 192 | bytes 1536
  426.9 1.9 collective-permute-start.1
  428.8 2.6 fusion.6
  433.0 4.9 %collective-permute-done.1 = f32[3,12]{0,1:T(8,128)} collective-permute-done((f32[3,12]{0,1:T(8,128)}, f32[3,12]{0,1:T(8,128)}, u32[]{:S(2)}, u32[]{:S(2)}) %collective-permute-start.1) | collective-permute-done | bytes 176 | tf_op jit(solution)/shard_map/ppermute | solution.py:791
  437.9 1.4 copy.72
  (122 shorter events, 28.1 us)
Async XLA Ops:
  0.6 6.5 %copy-start.16 = (bf16[864,96]{0,1:T(8,128)(2,1)S(1)}, bf16[864,96]{0,1:T(8,128)(2,1)}, u32[]{:S(2)}) copy-start(bf16[864,96]{0,1:T(8,128)(2,1)} %param.19) | copy-start | bytes 497668
  0.7 7.1 %copy-start.3 = (bf16[128,1536]{1,0:T(8,128)(2,1)S(1)}, bf16[128,1536]{1,0:T(8,128)(2,1)}, u32[]{:S(2)}) copy-start(bf16[128,1536]{1,0:T(8,128)(2,1)} %refs_0_.1) | copy-start | bytes 1179652
  0.7 7.3 %copy-start.32 = (bf16[96]{0:T(256)(128)(2,1)S(1)}, bf16[96]{0:T(256)(128)(2,1)}, u32[]{:S(2)}) copy-start(bf16[96]{0:T(256)(128)(2,1)} %param.12) | copy-start | bytes 580
  0.7 7.3 %copy-start.30 = (bf16[96]{0:T(256)(128)(2,1)S(1)}, bf16[96]{0:T(256)(128)(2,1)}, u32[]{:S(2)}) copy-start(bf16[96]{0:T(256)(128)(2,1)} %param.16) | copy-start | bytes 580
  0.7 7.3 %copy-start.6 = (bf16[128,1536]{1,0:T(8,128)(2,1)S(1)}, bf16[128,1536]{1,0:T(8,128)(2,1)}, u32[]{:S(2)}) copy-start(bf16[128,1536]{1,0:T(8,128)(2,1)} %param.21) | copy-start | bytes 1179652
  1.7 7.7 %copy-start.21 = (bf16[3,192]{1,0:T(4,128)(2,1)S(1)}, bf16[3,192]{1,0:T(4,128)(2,1)}, u32[]{:S(2)}) copy-start(bf16[3,192]{1,0:T(4,128)(2,1)} %param.14) | copy-start | bytes 3460
  8.0 220.4 %copy-start.19 = (f32[128]{0:T(128)}, f32[128]{0:T(128)S(1)}, u32[]{:S(2)}) copy-start(f32[128]{0:T(128)S(1)} %compare_convert_fusion) | copy-start | bytes 1540
  9.8 0.8 copy-start.17
  121.5 2.7 copy-start.5
  121.5 6.5 %copy-start.25 = (bf16[4,256,1792]{2,1,0:T(8,128)(2,1)S(1)}, bf16[4,256,1792]{2,1,0:T(8,128)(2,1)}, u32[]{:S(2)}) copy-start(bf16[4,256,1792]{2,1,0:T(8,128)(2,1)} %get-tuple-element.37) | copy-start | bytes 11010052
  187.0 6.5 %copy-start = (f32[128,1536]{1,0:T(8,128)S(1)}, f32[128,1536]{1,0:T(8,128)}, u32[]{:S(2)}) copy-start(f32[128,1536]{1,0:T(8,128)} %get-tuple-element.33) | copy-start | bytes 2359300
  227.0 3.6 copy-start.18
  228.4 2.2 copy-start.20
  230.6 6.5 %copy-start.1 = (f32[4,2,136,256]{3,2,1,0:T(8,128)S(1)}, f32[4,2,136,256]{3,2,1,0:T(8,128)}, u32[]{:S(2)}) copy-start(f32[4,2,136,256]{3,2,1,0:T(8,128)} %get-tuple-element.43) | copy-start | bytes 3342340
  244.8 33.2 %copy-start.9 = (f32[1024,192]{0,1:T(8,128)S(1)}, f32[1024,192]{0,1:T(8,128)}, u32[]{:S(2)}) copy-start(f32[1024,192]{0,1:T(8,128)} %copy.79) | copy-start | bytes 2359300
  244.8 33.2 %copy-start.10 = (f32[1024,192]{0,1:T(8,128)S(1)}, f32[1024,192]{0,1:T(8,128)}, u32[]{:S(2)}) copy-start(f32[1024,192]{0,1:T(8,128)} %copy.80) | copy-start | bytes 2359300
  283.2 5.7 %copy-start.31 = (bf16[96]{0:T(256)(128)(2,1)S(1)}, bf16[96]{0:T(256)(128)(2,1)}, u32[]{:S(2)}) copy-start(bf16[96]{0:T(256)(128)(2,1)} %param.16) | copy-start | bytes 580
  283.2 5.8 %copy-start.29 = (bf16[4,2,128,256]{3,2,1,0:T(8,128)(2,1)S(1)}, bf16[4,2,128,256]{3,2,1,0:T(8,128)(2,1)}, u32[]{:S(2)}) copy-start(bf16[4,2,128,256]{3,2,1,0:T(8,128)(2,1)} %get-tuple-element.49) | copy-start | bytes 1572868
  285.2 34.1 %collective-permute-start = (f32[4,2,2,192]{3,0,2,1:T(4,128)}, f32[4,2,2,192]{3,0,2,1:T(4,128)}, u32[]{:S(2)}, u32[]{:S(2)}) collective-permute-start(f32[4,2,2,192]{3,0,2,1:T(4,128)} %copy.77), channel_id=1, source_target_pairs={{0,1},{1,0},{2,3},{3,2},{4,5},{5,4},{6,7},{7,6},{8,9},{9,8},{10,11... | collective-permute-start | bytes 36872 | tf_op jit(solution)/shard_map/ppermute | solution.py:751
  289.0 3.8 copy-start.24
  289.0 3.7 copy-start.23
  289.0 3.7 copy-start.22
  289.0 3.8 copy-start.27
  289.0 3.8 copy-start.28
  292.8 5.7 %copy-start.12 = (bf16[96,3,192]{2,0,1:T(8,128)(2,1)S(1)}, bf16[96,3,192]{2,0,1:T(8,128)(2,1)}, u32[]{:S(2)}) copy-start(bf16[96,3,192]{2,0,1:T(8,128)(2,1)} %param.13) | copy-start | bytes 331780
  328.5 5.4 %copy-start.8 = (f32[1024,192]{0,1:T(8,128)S(1)}, f32[1024,192]{0,1:T(8,128)}, u32[]{:S(2)}) copy-start(f32[1024,192]{0,1:T(8,128)} %copy.78) | copy-start | bytes 2359300
  333.9 2.7 copy-start.15
  333.9 2.7 copy-start.26
  335.7 0.7 copy-start.13
  335.8 0.7 copy-start.14
  336.6 2.0 copy-start.11
  347.6 78.4 %copy-start.4 = (bf16[128,1536]{1,0:T(8,128)(2,1)S(1)}, bf16[128,1536]{1,0:T(8,128)(2,1)}, u32[]{:S(2)}) copy-start(bf16[128,1536]{1,0:T(8,128)(2,1)} %refs_0_.1) | copy-start | bytes 1179652
  392.8 33.2 %copy-start.7 = (f32[128,1536]{1,0:T(8,128)S(1)}, f32[128,1536]{1,0:T(8,128)}, u32[]{:S(2)}) copy-start(f32[128,1536]{1,0:T(8,128)} %get-tuple-element.51) | copy-start | bytes 2359300
  392.8 36.0 %copy-start.2 = (f32[128,1536]{1,0:T(8,128)S(1)}, f32[128,1536]{1,0:T(8,128)}, u32[]{:S(2)}) copy-start(f32[128,1536]{1,0:T(8,128)} %get-tuple-element.38) | copy-start | bytes 2359300
  426.9 11.0 %collective-permute-start.1 = (f32[3,12]{0,1:T(8,128)}, f32[3,12]{0,1:T(8,128)}, u32[]{:S(2)}, u32[]{:S(2)}) collective-permute-start(f32[3,12]{0,1:T(8,128)} %slice_bitcast_fusion.5), channel_id=1, source_target_pairs={{0,0},{1,16},{2,32},{3,48},{4,64},{5,80},{6,96},{7,112},{8,1},{9,1... | collective-permute-start | bytes 440 | tf_op jit(solution)/shard_map/ppermute | solution.py:791
